TPU v7x, 256 devices: a whole 4x4x8 slice. The times are simulated.
256 devices in a mesh: dp: 32 (over y, z), tensor: 8 (over x, core).
Axes of the slice: x: 4, y: 4, z: 8, core: 2. Of those that a mesh axis runs over, the one named last changes fastest.
Arguments:
- gradient: bfloat16 [32, 4096, 4096], P('dp', None, 'tensor'), may hold values from -6 to 6
- error: bfloat16 [32, 4096, 4096], P('dp', None, 'tensor'), may hold values from -4 to 4
- q_prev: float32 [4096, 64], P('tensor'), may hold values from -0.09375 to 0.09375
Outputs:
- q_new: float32 [4096, 64], P('tensor')
- new_error: bfloat16 [32, 4096, 4096], P('dp', None, 'tensor')
All inputs are finite; a program needn't handle non-finite values.
Results may differ from a plain program's by a relative error of at most 0.001.
Values sent between devices are 32-bit elements; how exact they have to be, the bound alone decides.
A program may use at most 64 MiB of HBM per device.

v0:
```python
import jax
import jax.numpy as jnp
from jax import lax
from jax.sharding import PartitionSpec as P

ITERS = 2


HIGH = lax.Precision.HIGHEST


def orthonormal(p_summed, factor):
    return lax.linalg.triangular_solve(
        factor, p_summed, left_side=False, lower=True, transpose_a=True
    )


def body(gradient, error, q_prev):
    merged = gradient[0].astype(jnp.float32) + error[0].astype(jnp.float32)
    inverse = 1.0 / lax.axis_size("dp")
    q_current = q_prev
    p_hat = None
    for sweep in range(ITERS):
        partial_p = jnp.dot(merged, q_current, precision=HIGH) * inverse
        p_summed = lax.psum(partial_p, ("dp", "tensor"))
        gram_matrix = jnp.dot(p_summed.T, p_summed, precision=HIGH)
        factor = jnp.linalg.cholesky(gram_matrix)
        p_hat = orthonormal(p_summed, factor)
        q_partial = jnp.dot(merged.T, p_hat, precision=HIGH)
        q_current = lax.psum(q_partial, "dp") * inverse
    approx = jnp.dot(p_hat, q_current.T, precision=HIGH)
    new_error = (merged - approx).astype(jnp.bfloat16)[None]
    return (q_current, new_error)


def solution(mesh):
    return jax.shard_map(
        body,
        mesh=mesh,
        in_specs=(P("dp", None, "tensor"), P("dp", None, "tensor"), P("tensor", None)),
        out_specs=(P("tensor", None), P("dp", None, "tensor")),
        check_vma=False,
    )
```

profile of v0, /device:TPU:2, one launch (start us, length us, event | category | flops | bytes accessed | tf_op | source)
XLA Modules:
  0.0 897.4 jit_solution(7573522547551101585)
XLA Ops:
  7.2 0.0 all-reduce.5.cloned.1.call-start
  7.2 0.8 copy-done
  8.1 12.3 %fusion.10 = f32[4096,64]{0,1:T(8,128)} fusion(f32[512,64]{0,1:T(8,128)S(1)} %copy-done, bf16[1,4096,512]{2,1,0:T(8,128)(2,1)} %param.7, bf16[1,4096,512]{2,1,0:T(8,128)(2,1)} %param.6), kind=kOutput, calls=%fused_computation.14 | convolution fusion | flops 1617166336 | bytes 9568256 | tf_op jit(solution)/shard_map/dot_general | solution.py:24
  20.4 0.0 all-reduce.5.cloned.1.call-update
  20.4 0.0 all-reduce.7.cloned.1.call-start
  20.5 259.0 %all-reduce.5.cloned.1.call-done = f32[4096,64]{0,1:T(8,128)} async-done(((f32[4096,64]{0,1:T(8,128)}), f32[4096,64]{0,1:T(8,128)}) %all-reduce.5.cloned.1.call-update) | async-done | bytes 1048592 | tf_op jit(solution)/shard_map/psum | solution.py:25
  279.4 2.5 fusion.27
  282.0 0.1 copy.5
  282.1 5.8 cholesky.44
  287.9 0.6 compare_reduce_fusion.1
  288.6 0.7 fusion.18
  289.2 4.9 custom-call.6
  294.1 2.3 convolution_bitcast_fusion.1
  296.4 9.2 %fusion.4 = f32[512,64]{0,1:T(8,128)} fusion(f32[4096,64]{0,1:T(8,128)S(1)} %convolution_bitcast_fusion.1, bf16[1,4096,512]{2,1,0:T(8,128)(2,1)} %param.7, bf16[1,4096,512]{2,1,0:T(8,128)(2,1)} %param.6), kind=kOutput, calls=%fused_computation.5 | convolution fusion | flops 1616904192 | bytes 9568256 | tf_op jit(solution)/shard_map/dot_general | solution.py:29
  305.6 0.0 all-reduce.7.cloned.1.call-update
  305.6 0.2 all-reduce.9.cloned.1.call-start
  305.8 139.3 %all-reduce.7.cloned.1.call-done = f32[512,64]{0,1:T(8,128)} async-done(((f32[512,64]{0,1:T(8,128)}), f32[512,64]{0,1:T(8,128)}) %all-reduce.7.cloned.1.call-update) | async-done | bytes 131088 | tf_op jit(solution)/shard_map/psum | solution.py:30
  445.1 13.4 %fusion.13 = f32[4096,64]{0,1:T(8,128)} fusion(bf16[1,4096,512]{2,1,0:T(8,128)(2,1)} %param.7, bf16[1,4096,512]{2,1,0:T(8,128)(2,1)} %param.6, f32[512,64]{0,1:T(8,128)} %all-reduce.7.cloned.1.call-done), kind=kOutput, calls=%fused_computation.15 | convolution fusion | flops 1617199104 | bytes 9568256 | tf_op jit(solution)/shard_map/dot_general | solution.py:24
  458.5 0.0 all-reduce.9.cloned.1.call-update
  458.5 0.3 all-reduce.11.cloned.1.call-start
  458.8 254.1 %all-reduce.9.cloned.1.call-done = f32[4096,64]{0,1:T(8,128)} async-done(((f32[4096,64]{0,1:T(8,128)}), f32[4096,64]{0,1:T(8,128)}) %all-reduce.9.cloned.1.call-update) | async-done | bytes 1048592 | tf_op jit(solution)/shard_map/psum | solution.py:25
  712.9 2.5 fusion.28
  715.4 0.1 copy.6
  715.5 5.8 cholesky.55
  721.4 0.6 compare_reduce_fusion
  722.0 0.7 fusion.19
  722.7 4.9 custom-call.7
  727.6 2.3 convolution_bitcast_fusion
  729.9 9.2 %fusion = f32[512,64]{0,1:T(8,128)} fusion(f32[4096,64]{0,1:T(8,128)S(1)} %convolution_bitcast_fusion, bf16[1,4096,512]{2,1,0:T(8,128)(2,1)} %param.7, bf16[1,4096,512]{2,1,0:T(8,128)(2,1)} %param.6), kind=kOutput, calls=%fused_computation.1 | convolution fusion | flops 1616904192 | bytes 9568256 | tf_op jit(solution)/shard_map/dot_general | solution.py:29
  739.1 139.6 %all-reduce.11.cloned.1.call-done = f32[512,64]{0,1:T(8,128)} async-done(((f32[512,64]{0,1:T(8,128)}), f32[512,64]{0,1:T(8,128)}) %all-reduce.11.cloned.1.call-update) | async-done | bytes 131088 | tf_op jit(solution)/shard_map/psum | solution.py:30
  878.6 0.9 broadcast_multiply_fusion
  879.6 11.3 %fusion.9 = bf16[1,4096,512]{2,1,0:T(8,128)(2,1)} fusion(f32[4096,64]{0,1:T(8,128)S(1)} %convolution_bitcast_fusion, f32[512,64]{0,1:T(8,128)S(1)} %broadcast_multiply_fusion, bf16[1,4096,512]{2,1,0:T(8,128)(2,1)} %param.7, bf16[1,4096,512]{2,1,0:T(8,128)(2,1)} %param.6), kind=kOutput, calls=%fused_computation.11 | convolution fusion | flops 1621098496 | bytes 13762560 | tf_op jit(solution)/shard_map/dot_general | solution.py:31
  (8 shorter events, 0.1 us)
Async XLA Ops:
  7.2 0.9 copy-start
  7.2 272.3 %all-reduce.5.cloned.1.call-start = ((), (), s32[]{:S(2)}) async-start(), calls=%async_computation | async-start | bytes 2097152 | tf_op jit(solution)/shard_map/psum | solution.py:25
  20.4 424.7 %all-reduce.7.cloned.1.call-start = ((), (), s32[]{:S(2)}) async-start(), calls=%async_computation.1 | async-start | bytes 262144 | tf_op jit(solution)/shard_map/psum | solution.py:30
  305.6 407.3 %all-reduce.9.cloned.1.call-start = ((), (), s32[]{:S(2)}) async-start(), calls=%async_computation.2 | async-start | bytes 2097152 | tf_op jit(solution)/shard_map/psum | solution.py:25
  458.5 420.1 %all-reduce.11.cloned.1.call-start = ((), (), s32[]{:S(2)}) async-start(), calls=%async_computation.3 | async-start | bytes 262144 | tf_op jit(solution)/shard_map/psum | solution.py:30
  879.5 11.3 %copy-start.1 = (f32[512,64]{0,1:T(8,128)}, f32[512,64]{0,1:T(8,128)S(1)}, u32[]{:S(2)}) copy-start(f32[512,64]{0,1:T(8,128)S(1)} %broadcast_multiply_fusion) | copy-start | bytes 393220
Sparse Core Ops, SparseCore 0:
  20.6 258.8 all-reduce.4
  305.7 139.3 all-reduce.6
  458.6 254.2 all-reduce.8
  739.2 139.3 all-reduce.10
where the time goes:
time: 898 us; the launch traced here: 897 us
  waiting for transfers between devices  792 us (88%)
  matrix products  64.9 us (7%)
  other arithmetic  25.1 us (3%)
  between operations  13.9 us (2%)
    psum x2, waiting for transfers between devices, body(): p_summed = lax.psum(partial_p, ('dp', 'tensor'))  513 us
    psum x2, waiting for transfers between devices, body(): q_current = lax.psum(q_partial, 'dp') * inverse  279 us
    dot_general x2, matrix products, body(): partial_p = jnp.dot(merged, q_current, precision=HIGH) * inverse  25.7 us
    dot_general x2, matrix products, body(): q_partial = jnp.dot(merged.T, p_hat, precision=HIGH)  18.3 us
  transfers between devices with their start and end apart: 4, of which 4 were waited for; matrix products, arithmetic and copies ran while one was open for 0% of the time, Pallas kernels for 0%

commit v1 on v0

v1 whole, which is shorter than its diff:
```python
import functools

import jax
import jax.numpy as jnp
from jax import lax
from jax.experimental import pallas as pl
from jax.experimental.pallas import tpu as pltpu
from jax.sharding import PartitionSpec as P

N = 4096
RANK = 64
ITERS = 2
NX, NY, NZ = 4, 4, 8
N_DP = NY * NZ
N_T = 2 * NX
COLS = N // N_T
CHUNK = N // N_T
LANES = 128
PIECES = 3
MESH = pl.DeviceIdType.MESH
HIGH = lax.Precision.HIGHEST
NT = (((1,), (1,)), ((), ()))


def ring_distance(step, size):
    return min(step % size, -step % size)


OFFSETS = sorted(
    [(dy, dz) for dy in range(NY) for dz in range(NZ) if dy or dz],
    key=lambda o: -(ring_distance(o[0], NY) + ring_distance(o[1], NZ)),
)


def split(value, pieces=PIECES):
    out = []
    for _ in range(pieces):
        piece = value.astype(jnp.bfloat16)
        out.append(piece)
        value = value - piece.astype(jnp.float32)
    return jnp.concatenate(out, axis=0)


def fold(value):
    total = value[0:RANK]
    for i in range(1, PIECES):
        total = total + value[i * RANK : (i + 1) * RANK]
    return total


def to_blocks(value):
    return jnp.concatenate(
        [value[:, l * LANES : (l + 1) * LANES].reshape(8, 8, LANES) for l in range(4)],
        axis=0,
    )


def from_blocks(value):
    return jnp.concatenate(
        [value[8 * l : 8 * l + 8].reshape(RANK, LANES) for l in range(4)], axis=1
    )


def eliminate(work, first, last):
    lane = lax.broadcasted_iota(jnp.int32, (RANK, 2 * RANK), 1)
    row = lax.broadcasted_iota(jnp.int32, (RANK, 1), 0)
    lane1 = lax.broadcasted_iota(jnp.int32, (1, 2 * RANK), 1)

    def step(j, carry):
        a = work[...]
        pivot_row = work[pl.ds(j, 1), :]
        pivot = jnp.sum(jnp.where(lane1 == j, pivot_row, 0.0), axis=1, keepdims=True)
        column = jnp.sum(jnp.where(lane == j, a, 0.0), axis=1, keepdims=True)
        column = jnp.where(row > j, column, 0.0)
        work[...] = a - column * (pivot_row / pivot)
        return carry

    lax.fori_loop(first, last, step, 0)


def inverse_factor(work):
    a = work[...]
    lane = lax.broadcasted_iota(jnp.int32, (RANK, 2 * RANK), 1)
    row = lax.broadcasted_iota(jnp.int32, (RANK, 2 * RANK), 0)
    diagonal = jnp.sum(jnp.where(lane == row, a, 0.0), axis=1, keepdims=True)
    return a[:, RANK:] / jnp.sqrt(diagonal)


def kernel(
    g_hbm, e_hbm, q_ref, q_out, new_out,
    g, e, qs, pp, sb, xs, xr, acc, yr, pg, qp, qr, qg, work, ph,
    load_sem, sib_send, sib_recv, x_send, x_recv, y_send, y_recv,
    ag_send, ag_recv, xg_send, xg_recv, sg_send, sg_recv,
    qr_send, qr_recv, qa_send, qa_recv,
):
    dp = lax.axis_index("dp")
    t = lax.axis_index("tensor")
    y, z = dp // NZ, dp % NZ
    x, c = t // 2, t % 2
    sibling = (dp, 2 * x + (1 - c))

    def dp_peer(o):
        return ((y + o[0]) % NY) * NZ + (z + o[1]) % NZ

    def x_at(d):
        return (x + d) % NX

    barrier = pltpu.get_barrier_semaphore()
    peers = [(dp_peer(o), t) for o in OFFSETS]
    everyone = peers + [sibling] + [(dp, 2 * x_at(d) + c) for d in (1, 2, 3)]
    for peer in everyone:
        pl.semaphore_signal(barrier, inc=1, device_id=peer, device_id_type=MESH)

    order = [2, 1, 3, 0]
    chunks = []
    for d in order:
        chunks += [2 * x_at(d) + (1 - c), 2 * x_at(d) + c]

    def rows_of(chunk):
        return pl.ds(pl.multiple_of(chunk * CHUNK, CHUNK), CHUNK)

    loads = []
    for i, chunk in enumerate(chunks):
        rows = rows_of(chunk)
        pair = []
        for k, (hbm, vmem) in enumerate(((g_hbm, g), (e_hbm, e))):
            copy = pltpu.make_async_copy(
                hbm.at[0, rows, :], vmem.at[rows, :], load_sem.at[i, k]
            )
            copy.start()
            pair.append(copy)
        loads.append(pair)

    qs[...] = split(q_ref[...])

    sends = []

    def send(src, dst, send_sem, recv_sem, device):
        copy = pltpu.make_async_remote_copy(
            src_ref=src,
            dst_ref=dst,
            send_sem=send_sem,
            recv_sem=recv_sem,
            device_id=device,
            device_id_type=MESH,
        )
        copy.start()
        return copy

    def wait_bytes(ref, sem):
        pltpu.make_async_copy(ref, ref, sem).wait()

    for it in range(ITERS):
        scale = 1.0 / N_DP

        def p_chunk(chunk):
            rows = rows_of(chunk)
            lhs = qs[...]
            a = lax.dot_general(lhs, g[rows, :], NT, preferred_element_type=jnp.float32)
            b = lax.dot_general(lhs, e[rows, :], NT, preferred_element_type=jnp.float32)
            return to_blocks(fold(a + b))

        def pass_on(d):
            wait_bytes(sb.at[it, d], sib_recv.at[it, d])
            total = xs[it, d] + sb[it, d]
            xs[it, d] = total
            if d:
                sends.append(
                    send(
                        xs.at[it, d],
                        xr.at[it, d - 1],
                        x_send.at[it, d - 1],
                        x_recv.at[it, d - 1],
                        (dp, 2 * x_at(d) + c),
                    )
                )

        for i, d in enumerate(order):
            if it == 0:
                loads[2 * i][0].wait()
                loads[2 * i][1].wait()
            pp[it, d] = p_chunk(chunks[2 * i])
            if it == 0 and i == 0:
                pl.semaphore_wait(barrier, len(everyone))
            sends.append(
                send(
                    pp.at[it, d],
                    sb.at[it, d],
                    sib_send.at[it, d],
                    sib_recv.at[it, d],
                    sibling,
                )
            )
            if it == 0:
                loads[2 * i + 1][0].wait()
                loads[2 * i + 1][1].wait()
            xs[it, d] = p_chunk(chunks[2 * i + 1])
            if i:
                pass_on(order[i - 1])
        pass_on(order[-1])

        total = xs[it, 0]
        for d in (1, 3, 2):
            wait_bytes(xr.at[it, d - 1], x_recv.at[it, d - 1])
            total = total + xr[it, d - 1]
        acc[it] = total * scale

        for k, peer in enumerate(peers):
            send(
                acc.at[it, peer[0]],
                yr.at[it, k],
                y_send.at[it],
                y_recv.at[it],
                peer,
            )
        own = acc[it, dp]
        wait_bytes(yr.at[it], y_recv.at[it])
        pg[it, t, dp] = own + jnp.sum(yr[it], axis=0)

        for peer in peers:
            send(
                pg.at[it, t, dp],
                pg.at[it, t, dp],
                ag_send.at[it],
                ag_recv.at[it],
                peer,
            )
        wait_bytes(yr.at[it], ag_recv.at[it])

        def share(d):
            slot = pg.at[it, 2 * x_at(-d) + c]
            return send(slot, slot, sg_send.at[it, d], sg_recv.at[it, d], sibling)

        for d in (2, 1, 3):
            sends.append(
                send(
                    pg.at[it, t],
                    pg.at[it, t],
                    xg_send.at[it, d - 1],
                    xg_recv.at[it, d - 1],
                    (dp, 2 * x_at(d) + c),
                )
            )
        sends.append(share(0))

        q_acc = jnp.zeros((RANK, COLS), jnp.float32)
        gram = jnp.zeros((PIECES * RANK, PIECES * RANK), jnp.float32)

        def q_chunk(chunk, q_acc, gram):
            rows = rows_of(chunk)
            lhs = split(from_blocks(pg[it, chunk]))
            a = jnp.dot(lhs, g[rows, :], preferred_element_type=jnp.float32)
            b = jnp.dot(lhs, e[rows, :], preferred_element_type=jnp.float32)
            more = lax.dot_general(lhs, lhs, NT, preferred_element_type=jnp.float32)
            return q_acc + fold(a + b), gram + more

        q_acc, gram = q_chunk(t, q_acc, gram)
        for d in (1, 3, 2):
            chunk = 2 * x_at(-d) + c
            wait_bytes(pg.at[it, chunk], xg_recv.at[it, d - 1])
            sends.append(share(d))
            q_acc, gram = q_chunk(chunk, q_acc, gram)
        for d in (0, 1, 3, 2):
            chunk = 2 * x_at(-d) + (1 - c)
            wait_bytes(pg.at[it, chunk], sg_recv.at[it, d])
            q_acc, gram = q_chunk(chunk, q_acc, gram)

        qp[it] = to_blocks(q_acc * scale)
        for k, peer in enumerate(peers):
            send(
                qp.at[it, peer[0]],
                qr.at[it, k],
                qr_send.at[it],
                qr_recv.at[it],
                peer,
            )

        square = jnp.zeros((RANK, RANK), jnp.float32)
        for i in range(PIECES):
            for j in range(PIECES):
                square = square + gram[
                    i * RANK : (i + 1) * RANK, j * RANK : (j + 1) * RANK
                ]
        row = lax.broadcasted_iota(jnp.int32, (RANK, RANK), 0)
        lane = lax.broadcasted_iota(jnp.int32, (RANK, RANK), 1)
        eye = jnp.where(row == lane, 1.0, 0.0)
        work[...] = jnp.concatenate([square, eye], axis=1)
        eliminate(work, 0, RANK // 2)

        wait_bytes(qr.at[it], qr_recv.at[it])
        qg[it, dp] = qp[it, dp] + jnp.sum(qr[it], axis=0)
        for peer in peers:
            send(
                qg.at[it, dp],
                qg.at[it, dp],
                qa_send.at[it],
                qa_recv.at[it],
                peer,
            )
        eliminate(work, RANK // 2, RANK)
        l_inverse = inverse_factor(work)

        if it == ITERS - 1:
            for chunk in range(N_T):
                p_t = from_blocks(pg[it, chunk])
                hat = jnp.dot(
                    l_inverse, p_t, precision=HIGH, preferred_element_type=jnp.float32
                )
                high = hat.astype(jnp.bfloat16).astype(jnp.float32)
                both = jnp.concatenate([high, hat - high], axis=0).T
                both = both.astype(jnp.bfloat16)
                ph[chunk * CHUNK : (chunk + 1) * CHUNK, :] = jnp.concatenate(
                    [both, both], axis=1
                )

        wait_bytes(qr.at[it], qa_recv.at[it])
        q_now = jnp.dot(
            l_inverse,
            from_blocks(qg[it]),
            precision=HIGH,
            preferred_element_type=jnp.float32,
        )
        if it < ITERS - 1:
            qs[...] = split(q_now)
        else:
            q_out[...] = q_now
            high = q_now.astype(jnp.bfloat16)
            low = (q_now - high.astype(jnp.float32)).astype(jnp.bfloat16)
            right = jnp.concatenate([high, high, low, low], axis=0)
            for chunk in range(N_T):
                rows = slice(chunk * CHUNK, (chunk + 1) * CHUNK)
                approx = jnp.dot(
                    ph[rows, :], right, preferred_element_type=jnp.float32
                )
                merged = g[rows, :].astype(jnp.float32) + e[rows, :].astype(jnp.float32)
                new_out[0, rows, :] = (merged - approx).astype(jnp.bfloat16)

    for copy in sends:
        copy.wait_send()
    for it in range(ITERS):
        for sem in (y_send, ag_send, qr_send, qa_send):
            wait_bytes(yr.at[it], sem.at[it])


def body(gradient, error, q_prev):
    f32, bf16 = jnp.float32, jnp.bfloat16
    blocks = (N_DP, 8, LANES)
    dma = pltpu.SemaphoreType.DMA
    vmem = pl.BlockSpec(memory_space=pltpu.VMEM)
    hbm = pl.BlockSpec(memory_space=pltpu.HBM)
    q_t, new_error = pl.pallas_call(
        kernel,
        out_shape=(
            jax.ShapeDtypeStruct((RANK, COLS), f32),
            jax.ShapeDtypeStruct((1, N, COLS), bf16),
        ),
        in_specs=[hbm, hbm, vmem],
        out_specs=(vmem, vmem),
        scratch_shapes=[
            pltpu.VMEM((N, COLS), bf16),
            pltpu.VMEM((N, COLS), bf16),
            pltpu.VMEM((PIECES * RANK, COLS), bf16),
            pltpu.VMEM((ITERS, NX, *blocks), f32),
            pltpu.VMEM((ITERS, NX, *blocks), f32),
            pltpu.VMEM((ITERS, NX, *blocks), f32),
            pltpu.VMEM((ITERS, NX - 1, *blocks), f32),
            pltpu.VMEM((ITERS, *blocks), f32),
            pltpu.VMEM((ITERS, N_DP - 1, 8, LANES), f32),
            pltpu.VMEM((ITERS, N_T, *blocks), f32),
            pltpu.VMEM((ITERS, *blocks), f32),
            pltpu.VMEM((ITERS, N_DP - 1, 8, LANES), f32),
            pltpu.VMEM((ITERS, *blocks), f32),
            pltpu.VMEM((RANK, 2 * RANK), f32),
            pltpu.VMEM((N, 4 * RANK), bf16),
            dma((N_T, 2)),
            dma((ITERS, NX)),
            dma((ITERS, NX)),
            dma((ITERS, NX - 1)),
            dma((ITERS, NX - 1)),
            dma((ITERS,)),
            dma((ITERS,)),
            dma((ITERS,)),
            dma((ITERS,)),
            dma((ITERS, NX - 1)),
            dma((ITERS, NX - 1)),
            dma((ITERS, NX)),
            dma((ITERS, NX)),
            dma((ITERS,)),
            dma((ITERS,)),
            dma((ITERS,)),
            dma((ITERS,)),
        ],
        compiler_params=pltpu.CompilerParams(
            collective_id=1, has_side_effects=True, vmem_limit_bytes=54 * 2**20
        ),
    )(gradient, error, q_prev.T)
    return q_t.T, new_error


def solution(mesh):
    return jax.shard_map(
        body,
        mesh=mesh,
        in_specs=(P("dp", None, "tensor"), P("dp", None, "tensor"), P("tensor", None)),
        out_specs=(P("tensor", None), P("dp", None, "tensor")),
        check_vma=False,
    )
```

time: 898 us -> 109 us (0.12)
  waiting for transfers between devices: 792 us -> 0 us
  Pallas kernels: 0 us -> 102 us
  matrix products: 64.9 us -> 0 us
  other arithmetic: 25.1 us -> 0 us
  between operations: 13.9 us -> 0.64 us
    psum x4 -> x0, waiting for transfers between devices: 792 us -> none  [the longest x2 513 us: body(): p_summed = lax.psum(partial_p, ('dp', 'tensor'))]
    pallas_call x0 -> x1, Pallas kernels: none -> 102 us  [body(): pl.pallas_call(kernel, out_shape=(jax.ShapeDtypeStruct((RANK, COLS), f32)...]
    dot_general x7 -> x0, matrix products: 60.4 us -> none  [the longest x2 25.7 us: body(): partial_p = jnp.dot(merged, q_current, precision=HIGH) * inverse]
    another operation x10 -> x0, other arithmetic: 24.1 us -> none  [the longest x6 13 us: body(): factor = jnp.linalg.cholesky(gram_matrix)]
  transfers between devices with their start and end apart: 4 -> 0, of which waited for: 4 -> 0; matrix products, arithmetic and copies ran while one was open for 0% -> 0% of each run, Pallas kernels for 0% -> 0%
where the time goes in v1:
time: 109 us
  Pallas kernels  102 us (94%)
  local copies, waits for them, and re-layouts  6.04 us (6%)
    pallas_call x1, Pallas kernels, body(): pl.pallas_call(kernel, out_shape=(jax.ShapeDtypeStruct((RANK, COLS), f32)...  102 us
    unnamed x2, local copies, waits for them, and re-layouts  6.04 us

profile of v1, /device:TPU:2, one launch (start us, length us, event | category | flops | bytes accessed | tf_op | source)
XLA Modules:
  0.0 109.0 jit_solution(9893613003139407537)
XLA Ops:
  0.6 102.3 %shard_map.50 = (f32[64,512]{1,0:T(8,128)}, bf16[1,4096,512]{2,1,0:T(8,128)(2,1)}) custom-call(bf16[1,4096,512]{2,1,0:T(8,128)(2,1)} %g_hbm.1, bf16[1,4096,512]{2,1,0:T(8,128)(2,1)} %e_hbm.1, f32[64,512]{1,0:T(8,128)} %bitcast.2), custom_call_target="tpu_custom_call" | custom-call | tf_op jit(solution)/shard_map/pallas_call | solution.py:351
  103.0 1.6 %copy.7 = f32[512,64]{0,1:T(8,128)} copy(f32[512,64]{0,1:T(8,128)} %bitcast.3) | data formatting | bytes 262144
  104.5 4.5 %copy.8 = bf16[1,4096,512]{2,1,0:T(8,128)(2,1)} copy(bf16[1,4096,512]{2,1,0:T(8,128)(2,1)} %get-tuple-element.9) | data formatting | bytes 8388608

commit v2 on v1

v2 whole, which is shorter than its diff:
```python
import functools

import jax
import jax.numpy as jnp
from jax import lax
from jax.experimental import pallas as pl
from jax.experimental.pallas import tpu as pltpu
from jax.sharding import PartitionSpec as P

N = 4096
RANK = 64
ITERS = 2
NX, NY, NZ = 4, 4, 8
N_DP = NY * NZ
N_T = 2 * NX
COLS = N // N_T
LANES = 128
PIECES = 3
MESH = pl.DeviceIdType.MESH
HIGH = lax.Precision.HIGHEST
NT = (((1,), (1,)), ((), ()))


def ring_distance(step, size):
    return min(step % size, -step % size)


def distance(o):
    return ring_distance(o[0], NY) + ring_distance(o[1], NZ)


OFFSETS = sorted(
    [(du, dz) for du in range(NY) for dz in range(NZ) if du or dz],
    key=lambda o: -distance(o),
)
FAR_FIRST = (4, 3, 5, 2, 6, 1, 7, 0)
NEAR_FIRST = FAR_FIRST[::-1]
GROUPS = 2 * NZ
ROWS = N // GROUPS


def split(value, pieces=PIECES):
    out = []
    for _ in range(pieces):
        piece = value.astype(jnp.bfloat16)
        out.append(piece)
        value = value - piece.astype(jnp.float32)
    return jnp.concatenate(out, axis=0)


def fold(value):
    total = value[0:RANK]
    for i in range(1, PIECES):
        total = total + value[i * RANK : (i + 1) * RANK]
    return total


def to_tiles(value):
    parts = [
        value[:, l * LANES : (l + 1) * LANES].reshape(8, 8, LANES)
        for l in range(value.shape[1] // LANES)
    ]
    return jnp.concatenate(parts, axis=0)


def from_tiles(value):
    parts = [
        value[8 * l : 8 * l + 8].reshape(RANK, LANES)
        for l in range(value.shape[0] // 8)
    ]
    return jnp.concatenate(parts, axis=1)


def eliminate(work, first, last):
    lane = lax.broadcasted_iota(jnp.int32, (RANK, 2 * RANK), 1)
    row = lax.broadcasted_iota(jnp.int32, (RANK, 1), 0)
    lane1 = lax.broadcasted_iota(jnp.int32, (1, 2 * RANK), 1)

    def step(j, carry):
        a = work[...]
        pivot_row = work[pl.ds(j, 1), :]
        pivot = jnp.sum(jnp.where(lane1 == j, pivot_row, 0.0), axis=1, keepdims=True)
        column = jnp.sum(jnp.where(lane == j, a, 0.0), axis=1, keepdims=True)
        column = jnp.where(row > j, column, 0.0)
        work[...] = a - column * (pivot_row / pivot)
        return carry

    lax.fori_loop(first, last, step, 0)


def inverse_factor(work):
    a = work[...]
    lane = lax.broadcasted_iota(jnp.int32, (RANK, 2 * RANK), 1)
    row = lax.broadcasted_iota(jnp.int32, (RANK, 2 * RANK), 0)
    diagonal = jnp.sum(jnp.where(lane == row, a, 0.0), axis=1, keepdims=True)
    return a[:, RANK:] / jnp.sqrt(diagonal)


def kernel(
    g_hbm, e_hbm, q_ref, q_out, new_out,
    g, e, qs, pp, sb, xs, xr, acc, yr, pg, qp, qr, qg, work, ph,
    load_sem, sib_send, sib_recv, x_send, x_recv, y_send, y_recv,
    ag_send, ag_recv, xg_send, xg_recv, sg_send, sg_recv,
    qr_send, qr_recv, qa_send, qa_recv,
):
    dp = lax.axis_index("dp")
    t = lax.axis_index("tensor")
    y, z = dp // NZ, dp % NZ
    x, c = t // 2, t % 2
    sibling = (dp, 2 * x + (1 - c))

    def device(y_at, z_at, x_at):
        return (y_at * NZ + z_at, 2 * x_at + c)

    def z_of(dz):
        return (z + dz) % NZ

    def line_place(z_at):
        odd = z_at % 2
        return x * (1 - odd) + y * odd

    def plane_place(z_at):
        odd = z_at % 2
        return y * (1 - odd) + x * odd

    def on_line(place, z_at):
        odd = z_at % 2
        return device(y * (1 - odd) + place * odd, z, place * (1 - odd) + x * odd)

    def on_plane(place, z_at, owner_z):
        odd = owner_z % 2
        return device(place * (1 - odd) + y * odd, z_at, x * (1 - odd) + place * odd)

    dp_peers = [device((y + o[0]) % NY, z_of(o[1]), x) for o in OFFSETS]
    others = [device(y, z_of(o[1]), (x + o[0]) % NX) for o in OFFSETS if o[0]]
    everyone = dp_peers + others + [sibling]

    def rows_of(core, z_at):
        return pl.ds(pl.multiple_of((core * NZ + z_at) * ROWS, ROWS), ROWS)

    loads = []
    for i, dz in enumerate(FAR_FIRST):
        for core in (1 - c, c):
            rows = rows_of(core, z_of(dz))
            pair = []
            for k, (hbm, vmem) in enumerate(((g_hbm, g), (e_hbm, e))):
                copy = pltpu.make_async_copy(
                    hbm.at[0, rows, :], vmem.at[rows, :], load_sem.at[len(loads), k]
                )
                copy.start()
                pair.append(copy)
            loads.append(pair)

    barrier = pltpu.get_barrier_semaphore()
    for peer in everyone:
        pl.semaphore_signal(barrier, inc=1, device_id=peer, device_id_type=MESH)

    qs[...] = split(q_ref[...])

    def send(src, dst, send_sem, recv_sem, target):
        pltpu.make_async_remote_copy(
            src_ref=src,
            dst_ref=dst,
            send_sem=send_sem,
            recv_sem=recv_sem,
            device_id=target,
            device_id_type=MESH,
        ).start()

    def wait_bytes(ref, sem):
        pltpu.make_async_copy(ref, ref, sem).wait()

    scale = 1.0 / N_DP
    for it in range(ITERS):

        def p_chunk(core, z_at):
            rows = rows_of(core, z_at)
            lhs = qs[...]
            a = lax.dot_general(lhs, g[rows, :], NT, preferred_element_type=jnp.float32)
            b = lax.dot_general(lhs, e[rows, :], NT, preferred_element_type=jnp.float32)
            return to_tiles(fold(a + b))

        def pass_along(dz):
            wait_bytes(sb.at[it, dz], sib_recv.at[it, dz])
            xs[it, dz] = xs[it, dz] + sb[it, dz]
            here = line_place(z_of(dz))
            for d in (2, 1, 3):
                place = (here + d) % NX
                send(
                    xs.at[it, dz, pl.ds(4 * place, 4)],
                    xr.at[it, dz, d - 1],
                    x_send.at[it],
                    x_recv.at[it, dz],
                    on_line(place, z_of(dz)),
                )

        for i, dz in enumerate(FAR_FIRST):
            if it == 0:
                for copy in loads[2 * i]:
                    copy.wait()
            pp[it, dz] = p_chunk(1 - c, z_of(dz))
            if it == 0 and i == 0:
                pl.semaphore_wait(barrier, len(everyone))
            send(
                pp.at[it, dz],
                sb.at[it, dz],
                sib_send.at[it],
                sib_recv.at[it, dz],
                sibling,
            )
            if it == 0:
                for copy in loads[2 * i + 1]:
                    copy.wait()
            xs[it, dz] = p_chunk(c, z_of(dz))
            if i:
                pass_along(FAR_FIRST[i - 1])
        pass_along(FAR_FIRST[-1])

        slot = 0
        for dz in FAR_FIRST:
            wait_bytes(xr.at[it, dz], x_recv.at[it, dz])
            total = xs[it, dz, pl.ds(4 * line_place(z_of(dz)), 4)]
            for d in (1, 2, 3):
                total = total + xr[it, dz, d - 1]
            acc[it, dz] = total * scale
            for du in (2, 1, 3, 0):
                if not (du or dz):
                    continue
                place = (plane_place(z_of(dz)) + du) % NY
                send(
                    acc.at[it, dz, place],
                    yr.at[it, slot],
                    y_send.at[it],
                    y_recv.at[it],
                    on_plane(place, z_of(dz), z_of(dz)),
                )
                slot += 1

        mine = 4 * line_place(z) + plane_place(z)
        own = acc[it, 0, plane_place(z)]
        wait_bytes(yr.at[it], y_recv.at[it])
        pg[it, c * NZ + z, mine] = own + jnp.sum(yr[it], axis=0)

        for du, dz in OFFSETS:
            tile = pg.at[it, c * NZ + z, mine]
            place = (plane_place(z) + du) % NY
            send(
                tile,
                tile,
                ag_send.at[it],
                ag_recv.at[it, dz],
                on_plane(place, z_of(dz), z),
            )

        for dz in NEAR_FIRST:
            z_at = z_of(-dz)
            here = line_place(z_at)
            tiles = pg.at[it, c * NZ + z_at, pl.ds(4 * here, 4)]
            if dz:
                wait_bytes(tiles, ag_recv.at[it, dz])
            else:
                wait_bytes(yr.at[it, pl.ds(0, 3)], ag_recv.at[it, dz])
            for d in (2, 1, 3):
                send(
                    tiles,
                    tiles,
                    xg_send.at[it],
                    xg_recv.at[it, dz],
                    on_line((here + d) % NX, z_at),
                )

        q_acc = jnp.zeros((RANK, COLS), jnp.float32)
        gram = jnp.zeros((PIECES * RANK, PIECES * RANK), jnp.float32)

        def q_chunk(core, z_at, q_acc, gram):
            rows = rows_of(core, z_at)
            lhs = split(from_tiles(pg[it, core * NZ + z_at]))
            a = jnp.dot(lhs, g[rows, :], preferred_element_type=jnp.float32)
            b = jnp.dot(lhs, e[rows, :], preferred_element_type=jnp.float32)
            more = lax.dot_general(lhs, lhs, NT, preferred_element_type=jnp.float32)
            return q_acc + fold(a + b), gram + more

        for dz in NEAR_FIRST:
            z_at = z_of(-dz)
            wait_bytes(xr.at[it, 0], xg_recv.at[it, dz])
            chunk = pg.at[it, c * NZ + z_at]
            send(chunk, chunk, sg_send.at[it], sg_recv.at[it, dz], sibling)
            q_acc, gram = q_chunk(c, z_at, q_acc, gram)
        for dz in NEAR_FIRST:
            z_at = z_of(-dz)
            wait_bytes(pg.at[it, (1 - c) * NZ + z_at], sg_recv.at[it, dz])
            q_acc, gram = q_chunk(1 - c, z_at, q_acc, gram)

        qp[it] = to_tiles(q_acc * scale)
        for k, peer in enumerate(dp_peers):
            send(
                qp.at[it, peer[0]],
                qr.at[it, k],
                qr_send.at[it],
                qr_recv.at[it],
                peer,
            )

        square = jnp.zeros((RANK, RANK), jnp.float32)
        for i in range(PIECES):
            for j in range(PIECES):
                square = square + gram[
                    i * RANK : (i + 1) * RANK, j * RANK : (j + 1) * RANK
                ]
        row = lax.broadcasted_iota(jnp.int32, (RANK, RANK), 0)
        lane = lax.broadcasted_iota(jnp.int32, (RANK, RANK), 1)
        eye = jnp.where(row == lane, 1.0, 0.0)
        work[...] = jnp.concatenate([square, eye], axis=1)
        eliminate(work, 0, RANK // 2)

        wait_bytes(qr.at[it], qr_recv.at[it])
        qg[it, dp] = qp[it, dp] + jnp.sum(qr[it], axis=0)
        for peer in dp_peers:
            send(
                qg.at[it, dp],
                qg.at[it, dp],
                qa_send.at[it],
                qa_recv.at[it],
                peer,
            )
        eliminate(work, RANK // 2, RANK)
        l_inverse = inverse_factor(work)

        if it == ITERS - 1:
            for i in range(GROUPS):
                hat = jnp.dot(
                    l_inverse,
                    from_tiles(pg[it, i]),
                    precision=HIGH,
                    preferred_element_type=jnp.float32,
                )
                high = hat.astype(jnp.bfloat16).astype(jnp.float32)
                both = jnp.concatenate([high, hat - high], axis=0).T
                both = both.astype(jnp.bfloat16)
                ph[i * ROWS : (i + 1) * ROWS, :] = jnp.concatenate([both, both], axis=1)

        wait_bytes(pp.at[it], sib_send.at[it])
        wait_bytes(xr.at[it], x_send.at[it])
        wait_bytes(yr.at[it], y_send.at[it])
        wait_bytes(yr.at[it], ag_send.at[it])
        wait_bytes(xr.at[it], xg_send.at[it])
        wait_bytes(pp.at[it], sg_send.at[it])
        wait_bytes(qr.at[it], qr_send.at[it])

        wait_bytes(qr.at[it], qa_recv.at[it])
        q_now = jnp.dot(
            l_inverse,
            from_tiles(qg[it]),
            precision=HIGH,
            preferred_element_type=jnp.float32,
        )
        if it < ITERS - 1:
            qs[...] = split(q_now)
        else:
            q_out[...] = q_now
            high = q_now.astype(jnp.bfloat16)
            low = (q_now - high.astype(jnp.float32)).astype(jnp.bfloat16)
            right = jnp.concatenate([high, high, low, low], axis=0)
            for i in range(N_T):
                rows = slice(i * COLS, (i + 1) * COLS)
                approx = jnp.dot(
                    ph[rows, :], right, preferred_element_type=jnp.float32
                )
                merged = g[rows, :].astype(jnp.float32) + e[rows, :].astype(jnp.float32)
                new_out[0, rows, :] = (merged - approx).astype(jnp.bfloat16)

    for it in range(ITERS):
        wait_bytes(qr.at[it], qa_send.at[it])


def body(gradient, error, q_prev):
    f32, bf16 = jnp.float32, jnp.bfloat16
    dma = pltpu.SemaphoreType.DMA
    vmem = pl.BlockSpec(memory_space=pltpu.VMEM)
    hbm = pl.BlockSpec(memory_space=pltpu.HBM)
    q_t, new_error = pl.pallas_call(
        kernel,
        out_shape=(
            jax.ShapeDtypeStruct((RANK, COLS), f32),
            jax.ShapeDtypeStruct((1, N, COLS), bf16),
        ),
        in_specs=[hbm, hbm, vmem],
        out_specs=(vmem, vmem),
        scratch_shapes=[
            pltpu.VMEM((N, COLS), bf16),
            pltpu.VMEM((N, COLS), bf16),
            pltpu.VMEM((PIECES * RANK, COLS), bf16),
            pltpu.VMEM((ITERS, NZ, 16, 8, LANES), f32),
            pltpu.VMEM((ITERS, NZ, 16, 8, LANES), f32),
            pltpu.VMEM((ITERS, NZ, 16, 8, LANES), f32),
            pltpu.VMEM((ITERS, NZ, 3, 4, 8, LANES), f32),
            pltpu.VMEM((ITERS, NZ, 4, 8, LANES), f32),
            pltpu.VMEM((ITERS, N_DP - 1, 8, LANES), f32),
            pltpu.VMEM((ITERS, GROUPS, 16, 8, LANES), f32),
            pltpu.VMEM((ITERS, N_DP, 8, LANES), f32),
            pltpu.VMEM((ITERS, N_DP - 1, 8, LANES), f32),
            pltpu.VMEM((ITERS, N_DP, 8, LANES), f32),
            pltpu.VMEM((RANK, 2 * RANK), f32),
            pltpu.VMEM((N, 4 * RANK), bf16),
            dma((GROUPS, 2)),
            dma((ITERS,)),
            dma((ITERS, NZ)),
            dma((ITERS,)),
            dma((ITERS, NZ)),
            dma((ITERS,)),
            dma((ITERS,)),
            dma((ITERS,)),
            dma((ITERS, NZ)),
            dma((ITERS,)),
            dma((ITERS, NZ)),
            dma((ITERS,)),
            dma((ITERS, NZ)),
            dma((ITERS,)),
            dma((ITERS,)),
            dma((ITERS,)),
            dma((ITERS,)),
        ],
        compiler_params=pltpu.CompilerParams(
            collective_id=1, has_side_effects=True, vmem_limit_bytes=48 * 2**20
        ),
    )(gradient, error, q_prev.T)
    return q_t.T, new_error


def solution(mesh):
    return jax.shard_map(
        body,
        mesh=mesh,
        in_specs=(P("dp", None, "tensor"), P("dp", None, "tensor"), P("tensor", None)),
        out_specs=(P("tensor", None), P("dp", None, "tensor")),
        check_vma=False,
    )
```

time: 109 us -> 95.6 us (0.88)
  Pallas kernels: 102 us -> 91.3 us
  local copies, waits for them, and re-layouts: 6.04 us -> 3.57 us
    pallas_call x1, Pallas kernels: 102 us -> 91.3 us  [body(): pl.pallas_call(kernel, out_shape=(jax.ShapeDtypeStruct((RANK, COLS), f32)...]
    unnamed x2 -> x4, local copies, waits for them, and re-layouts: 6.04 us -> 3.57 us
where the time goes in v2:
time: 95.6 us; the launch traced here: 95.5 us
  Pallas kernels  91.3 us (96%)
  local copies, waits for them, and re-layouts  3.57 us (4%)
    pallas_call x1, Pallas kernels, body(): pl.pallas_call(kernel, out_shape=(jax.ShapeDtypeStruct((RANK, COLS), f32)...  91.3 us
    unnamed x4, local copies, waits for them, and re-layouts  3.57 us

profile of v2, /device:TPU:2, one launch (start us, length us, event | category | flops | bytes accessed | tf_op | source)
XLA Modules:
  0.0 95.5 jit_solution(3367664448089932054)
XLA Ops:
  0.6 0.0 copy-start
  0.6 0.9 copy-done
  1.5 91.3 %shard_map.50 = (f32[64,512]{1,0:T(8,128)S(1)}, bf16[1,4096,512]{2,1,0:T(8,128)(2,1)S(1)}) custom-call(bf16[1,4096,512]{2,1,0:T(8,128)(2,1)} %g_hbm.1, bf16[1,4096,512]{2,1,0:T(8,128)(2,1)} %e_hbm.1, f32[64,512]{1,0:T(8,128)S(1)} %bitcast.2), custom_call_target="tpu_custom_call" | custom-call | tf_op jit(solution)/shard_map/pallas_call | solution.py:381
  92.8 0.7 copy.7
  93.5 2.0 %copy.8 = bf16[1,4096,512]{2,1,0:T(8,128)(2,1)} copy(bf16[1,4096,512]{2,1,0:T(8,128)(2,1)S(1)} %get-tuple-element.9) | data formatting | bytes 8388608
Async XLA Ops:
  0.6 0.9 copy-start

commit v3 on v2

--- a/solution.py
+++ b/solution.py
@@ -39,13 +39,38 @@
 ROWS = N // GROUPS
 
 
-def split(value, pieces=PIECES):
+def pieces_of(value):
     out = []
-    for _ in range(pieces):
-        piece = value.astype(jnp.bfloat16)
+    for _ in range(PIECES):
+        piece = value.astype(jnp.bfloat16).astype(jnp.float32)
         out.append(piece)
-        value = value - piece.astype(jnp.float32)
-    return jnp.concatenate(out, axis=0)
+        value = value - piece
+    return out
+
+
+def split(value):
+    return jnp.concatenate([p.astype(jnp.bfloat16) for p in pieces_of(value)], axis=0)
+
+
+def right_factor(q_t):
+    high, mid, low = pieces_of(q_t)
+    first = jnp.concatenate([high, mid], axis=0).T
+    second = jnp.concatenate([low, jnp.zeros_like(low)], axis=0).T
+    return jnp.concatenate([first, second], axis=1).astype(jnp.bfloat16)
+
+
+def pack(value):
+    both = value[:, :LANES] + value[:, LANES:]
+    top, bottom = both[:LANES], both[LANES:]
+    lower = lax.broadcasted_iota(jnp.int32, (LANES, LANES), 1) < RANK
+    kept = jnp.where(lower, top, bottom)
+    moved = pltpu.roll(jnp.where(lower, bottom, top), RANK, 1)
+    return (kept + moved).reshape(16, 8, LANES)
+
+
+def unpack_transposed(tiles):
+    value = tiles.reshape(LANES, LANES).T
+    return jnp.concatenate([value[:RANK], value[RANK:]], axis=1)
 
 
 def fold(value):
@@ -97,8 +122,8 @@
 
 
 def kernel(
-    g_hbm, e_hbm, q_ref, q_out, new_out,
-    g, e, qs, pp, sb, xs, xr, acc, yr, pg, qp, qr, qg, work, ph,
+    g_hbm, e_hbm, q_ref, q_out, g, e, ph,
+    qs, pp, sb, xs, xr, acc, yr, pg, qp, qr, qg, work,
     load_sem, sib_send, sib_recv, x_send, x_recv, y_send, y_recv,
     ag_send, ag_recv, xg_send, xg_recv, sg_send, sg_recv,
     qr_send, qr_recv, qa_send, qa_recv,
@@ -133,7 +158,16 @@
 
     dp_peers = [device((y + o[0]) % NY, z_of(o[1]), x) for o in OFFSETS]
     others = [device(y, z_of(o[1]), (x + o[0]) % NX) for o in OFFSETS if o[0]]
-    everyone = dp_peers + others + [sibling]
+    near_x = [o for o in OFFSETS if o[0]]
+    by_distance = sorted(
+        list(zip(OFFSETS, dp_peers)) + list(zip(near_x, others)),
+        key=lambda pair: -distance(pair[0]),
+    )
+    everyone = [peer for _, peer in by_distance] + [sibling]
+
+    barrier = pltpu.get_barrier_semaphore()
+    for peer in everyone:
+        pl.semaphore_signal(barrier, inc=1, device_id=peer, device_id_type=MESH)
 
     def rows_of(core, z_at):
         return pl.ds(pl.multiple_of((core * NZ + z_at) * ROWS, ROWS), ROWS)
@@ -151,11 +185,7 @@
                 pair.append(copy)
             loads.append(pair)
 
-    barrier = pltpu.get_barrier_semaphore()
-    for peer in everyone:
-        pl.semaphore_signal(barrier, inc=1, device_id=peer, device_id_type=MESH)
-
-    qs[...] = split(q_ref[...])
+    qs[...] = right_factor(q_ref[...])
 
     def send(src, dst, send_sem, recv_sem, target):
         pltpu.make_async_remote_copy(
@@ -175,10 +205,10 @@
 
         def p_chunk(core, z_at):
             rows = rows_of(core, z_at)
-            lhs = qs[...]
-            a = lax.dot_general(lhs, g[rows, :], NT, preferred_element_type=jnp.float32)
-            b = lax.dot_general(lhs, e[rows, :], NT, preferred_element_type=jnp.float32)
-            return to_tiles(fold(a + b))
+            factor = qs[...]
+            a = jnp.dot(g[rows, :], factor, preferred_element_type=jnp.float32)
+            b = jnp.dot(e[rows, :], factor, preferred_element_type=jnp.float32)
+            return pack(a + b)
 
         def pass_along(dz):
             wait_bytes(sb.at[it, dz], sib_recv.at[it, dz])
@@ -194,13 +224,7 @@
                     on_line(place, z_of(dz)),
                 )
 
-        for i, dz in enumerate(FAR_FIRST):
-            if it == 0:
-                for copy in loads[2 * i]:
-                    copy.wait()
-            pp[it, dz] = p_chunk(1 - c, z_of(dz))
-            if it == 0 and i == 0:
-                pl.semaphore_wait(barrier, len(everyone))
+        def to_sibling(dz):
             send(
                 pp.at[it, dz],
                 sb.at[it, dz],
@@ -208,13 +232,26 @@
                 sib_recv.at[it, dz],
                 sibling,
             )
-            if it == 0:
-                for copy in loads[2 * i + 1]:
+
+        if it == 0:
+            for i, dz in enumerate(FAR_FIRST):
+                for copy in loads[2 * i] + loads[2 * i + 1]:
                     copy.wait()
-            xs[it, dz] = p_chunk(c, z_of(dz))
-            if i:
-                pass_along(FAR_FIRST[i - 1])
-        pass_along(FAR_FIRST[-1])
+                pp[it, dz] = p_chunk(1 - c, z_of(dz))
+                xs[it, dz] = p_chunk(c, z_of(dz))
+            pl.semaphore_wait(barrier, len(everyone))
+            for dz in FAR_FIRST:
+                to_sibling(dz)
+            for dz in FAR_FIRST:
+                pass_along(dz)
+        else:
+            for i, dz in enumerate(FAR_FIRST):
+                pp[it, dz] = p_chunk(1 - c, z_of(dz))
+                to_sibling(dz)
+                xs[it, dz] = p_chunk(c, z_of(dz))
+                if i:
+                    pass_along(FAR_FIRST[i - 1])
+            pass_along(FAR_FIRST[-1])
 
         slot = 0
         for dz in FAR_FIRST:
@@ -274,7 +311,7 @@
 
         def q_chunk(core, z_at, q_acc, gram):
             rows = rows_of(core, z_at)
-            lhs = split(from_tiles(pg[it, core * NZ + z_at]))
+            lhs = split(unpack_transposed(pg[it, core * NZ + z_at]))
             a = jnp.dot(lhs, g[rows, :], preferred_element_type=jnp.float32)
             b = jnp.dot(lhs, e[rows, :], preferred_element_type=jnp.float32)
             more = lax.dot_general(lhs, lhs, NT, preferred_element_type=jnp.float32)
@@ -327,16 +364,28 @@
         l_inverse = inverse_factor(work)
 
         if it == ITERS - 1:
+            none = jnp.zeros((RANK, RANK), jnp.float32)
+            twice = jnp.concatenate(
+                [
+                    jnp.concatenate([l_inverse, none], axis=1),
+                    jnp.concatenate([none, l_inverse], axis=1),
+                ],
+                axis=0,
+            )
+            lower = lax.broadcasted_iota(jnp.int32, (LANES, LANES), 1) < RANK
             for i in range(GROUPS):
-                hat = jnp.dot(
-                    l_inverse,
-                    from_tiles(pg[it, i]),
+                hat = lax.dot_general(
+                    pg[it, i].reshape(LANES, LANES),
+                    twice,
+                    NT,
                     precision=HIGH,
                     preferred_element_type=jnp.float32,
                 )
                 high = hat.astype(jnp.bfloat16).astype(jnp.float32)
-                both = jnp.concatenate([high, hat - high], axis=0).T
-                both = both.astype(jnp.bfloat16)
+                low = hat - high
+                top = jnp.where(lower, high, pltpu.roll(low, RANK, 1))
+                bottom = jnp.where(lower, pltpu.roll(high, RANK, 1), low)
+                both = jnp.concatenate([top, bottom], axis=0).astype(jnp.bfloat16)
                 ph[i * ROWS : (i + 1) * ROWS, :] = jnp.concatenate([both, both], axis=1)
 
         wait_bytes(pp.at[it], sib_send.at[it])
@@ -355,22 +404,29 @@
             preferred_element_type=jnp.float32,
         )
         if it < ITERS - 1:
-            qs[...] = split(q_now)
+            qs[...] = right_factor(q_now)
         else:
             q_out[...] = q_now
-            high = q_now.astype(jnp.bfloat16)
-            low = (q_now - high.astype(jnp.float32)).astype(jnp.bfloat16)
-            right = jnp.concatenate([high, high, low, low], axis=0)
-            for i in range(N_T):
-                rows = slice(i * COLS, (i + 1) * COLS)
-                approx = jnp.dot(
-                    ph[rows, :], right, preferred_element_type=jnp.float32
-                )
-                merged = g[rows, :].astype(jnp.float32) + e[rows, :].astype(jnp.float32)
-                new_out[0, rows, :] = (merged - approx).astype(jnp.bfloat16)
 
     for it in range(ITERS):
         wait_bytes(qr.at[it], qa_send.at[it])
+
+
+def finish(g, e, ph, q_ref, q_out, new_out, right):
+    step = pl.program_id(0)
+
+    @pl.when(step == 0)
+    def _():
+        q_now = q_ref[...]
+        q_out[...] = q_now
+        high = q_now.astype(jnp.bfloat16)
+        low = (q_now - high.astype(jnp.float32)).astype(jnp.bfloat16)
+        right[...] = jnp.concatenate([high, high, low, low], axis=0)
+
+    rows = pl.ds(pl.multiple_of(step * COLS, COLS), COLS)
+    approx = jnp.dot(ph[rows, :], right[...], preferred_element_type=jnp.float32)
+    merged = g[rows, :].astype(jnp.float32) + e[rows, :].astype(jnp.float32)
+    new_out[0] = (merged - approx).astype(jnp.bfloat16)
 
 
 def body(gradient, error, q_prev):
@@ -378,18 +434,18 @@
     dma = pltpu.SemaphoreType.DMA
     vmem = pl.BlockSpec(memory_space=pltpu.VMEM)
     hbm = pl.BlockSpec(memory_space=pltpu.HBM)
-    q_t, new_error = pl.pallas_call(
+    q_t, g, e, p_hat = pl.pallas_call(
         kernel,
         out_shape=(
             jax.ShapeDtypeStruct((RANK, COLS), f32),
-            jax.ShapeDtypeStruct((1, N, COLS), bf16),
+            jax.ShapeDtypeStruct((N, COLS), bf16),
+            jax.ShapeDtypeStruct((N, COLS), bf16),
+            jax.ShapeDtypeStruct((N, 4 * RANK), bf16),
         ),
         in_specs=[hbm, hbm, vmem],
-        out_specs=(vmem, vmem),
+        out_specs=(vmem, vmem, vmem, vmem),
         scratch_shapes=[
-            pltpu.VMEM((N, COLS), bf16),
-            pltpu.VMEM((N, COLS), bf16),
-            pltpu.VMEM((PIECES * RANK, COLS), bf16),
+            pltpu.VMEM((COLS, 4 * RANK), bf16),
             pltpu.VMEM((ITERS, NZ, 16, 8, LANES), f32),
             pltpu.VMEM((ITERS, NZ, 16, 8, LANES), f32),
             pltpu.VMEM((ITERS, NZ, 16, 8, LANES), f32),
@@ -401,7 +457,6 @@
             pltpu.VMEM((ITERS, N_DP - 1, 8, LANES), f32),
             pltpu.VMEM((ITERS, N_DP, 8, LANES), f32),
             pltpu.VMEM((RANK, 2 * RANK), f32),
-            pltpu.VMEM((N, 4 * RANK), bf16),
             dma((GROUPS, 2)),
             dma((ITERS,)),
             dma((ITERS, NZ)),
@@ -421,9 +476,24 @@
             dma((ITERS,)),
         ],
         compiler_params=pltpu.CompilerParams(
-            collective_id=1, has_side_effects=True, vmem_limit_bytes=48 * 2**20
+            collective_id=1, has_side_effects=True, vmem_limit_bytes=41 * 2**20
         ),
     )(gradient, error, q_prev.T)
+    q_t, new_error = pl.pallas_call(
+        finish,
+        grid=(N // COLS,),
+        out_shape=(
+            jax.ShapeDtypeStruct((RANK, COLS), f32),
+            jax.ShapeDtypeStruct((1, N, COLS), bf16),
+        ),
+        in_specs=[vmem, vmem, vmem, vmem],
+        out_specs=(
+            pl.BlockSpec((RANK, COLS), lambda i: (0, 0)),
+            pl.BlockSpec((1, COLS, COLS), lambda i: (0, i, 0)),
+        ),
+        scratch_shapes=[pltpu.VMEM((4 * RANK, COLS), bf16)],
+        compiler_params=pltpu.CompilerParams(vmem_limit_bytes=24 * 2**20),
+    )(g, e, p_hat, q_t)
     return q_t.T, new_error
 
 

time: 95.6 us -> 96.1 us (level)
  Pallas kernels: 91.3 us -> 94.4 us
  local copies, waits for them, and re-layouts: 3.57 us -> 0.9 us
    pallas_call x0 -> x1, Pallas kernels: none -> 4.75 us  [body(): pl.pallas_call(finish, grid=(N // COLS,), out_shape=(jax.ShapeDtypeStruct...]
    unnamed x4 -> x2, local copies, waits for them, and re-layouts: 3.57 us -> 0.9 us
    pallas_call x1, Pallas kernels: 91.3 us -> 89.6 us  [body(): pl.pallas_call(kernel, out_shape=(jax.ShapeDtypeStruct((RANK, COLS), f32)...]
where the time goes in v3:
time: 96.1 us; the launch traced here: 95.9 us
  Pallas kernels  94.4 us (98%)
    pallas_call x1, Pallas kernels, body(): pl.pallas_call(kernel, out_shape=(jax.ShapeDtypeStruct((RANK, COLS), f32)...  89.6 us
    pallas_call x1, Pallas kernels, body(): pl.pallas_call(finish, grid=(N // COLS,), out_shape=(jax.ShapeDtypeStruct...  4.75 us

profile of v3, /device:TPU:2, one launch (start us, length us, event | category | flops | bytes accessed | tf_op | source)
XLA Modules:
  0.0 95.9 jit_solution(18019945642490509104)
XLA Ops:
  0.6 0.0 copy-start
  0.6 0.9 copy-done
  1.5 89.6 %shard_map.50 = (f32[64,512]{1,0:T(8,128)S(1)}, bf16[4096,512]{1,0:T(8,128)(2,1)S(1)}, bf16[4096,512]{1,0:T(8,128)(2,1)S(1)}, bf16[4096,256]{1,0:T(8,128)(2,1)S(1)}) custom-call(bf16[1,4096,512]{2,1,0:T(8,128)(2,1)} %g_hbm.1, bf16[1,4096,512]{2,1,0:T(8,128)(2,1)} %e_hbm.1, f32[64,512]{1,0:T(8,128)S(1)} %bitcast.2), custom_call_target="tpu_custom_call" | custom-call | tf_op jit(solution)/shard_map/pallas_call | solution.py:437
  91.1 4.8 %shard_map.51 = (f32[64,512]{1,0:T(8,128)}, bf16[1,4096,512]{2,1,0:T(8,128)(2,1)}) custom-call(bf16[4096,512]{1,0:T(8,128)(2,1)S(1)} %get-tuple-element.8.g, bf16[4096,512]{1,0:T(8,128)(2,1)S(1)} %get-tuple-element.9.e, bf16[4096,256]{1,0:T(8,128)(2,1)S(1)} %get-tuple-element.10.ph, f32[64,512]{1,0:T(8,128)S(1)} %get-tuple-element.11.q_ref), custom_call_target="tpu_custom_call" | custom-call | tf_op jit(solution)/shard_map/pallas_call | solution.py:482
Async XLA Ops:
  0.6 0.9 copy-start

commit v4 on v3

v4 whole, which is shorter than its diff:
```python
import functools

import jax
import jax.numpy as jnp
from jax import lax
from jax.experimental import pallas as pl
from jax.experimental.pallas import tpu as pltpu
from jax.sharding import PartitionSpec as P

N = 4096
RANK = 64
ITERS = 2
NX, NY, NZ = 4, 4, 8
N_DP = NY * NZ
N_T = 2 * NX
COLS = N // N_T
LANES = 128
PIECES = 3
EARLY = 48
MESH = pl.DeviceIdType.MESH
HIGH = lax.Precision.HIGHEST
NT = (((1,), (1,)), ((), ()))


def ring_distance(step, size):
    return min(step % size, -step % size)


def distance(o):
    return ring_distance(o[0], NY) + ring_distance(o[1], NZ)


OFFSETS = sorted(
    [(du, dz) for du in range(NY) for dz in range(NZ) if du or dz],
    key=lambda o: -distance(o),
)
SLOTS = (4, 3, 5, 2, 6, 1, 7, 0)
SPANS = ((0, 1), (1, 3), (3, 5), (5, 7), (7, 8))
N_SPANS = len(SPANS)
ROWS = N // (2 * NZ)


def slot_of(dz):
    return SLOTS.index(dz % NZ)


def span_of(dz):
    return N_SPANS - 1 - ring_distance(dz, NZ)


def pieces_of(value):
    out = []
    for _ in range(PIECES):
        piece = value.astype(jnp.bfloat16).astype(jnp.float32)
        out.append(piece)
        value = value - piece
    return out


def split(value):
    return jnp.concatenate([p.astype(jnp.bfloat16) for p in pieces_of(value)], axis=0)


def right_factor(q_t):
    high, mid, low = pieces_of(q_t)
    first = jnp.concatenate([high, mid], axis=0).T
    second = jnp.concatenate([low, jnp.zeros_like(low)], axis=0).T
    return jnp.concatenate([first, second], axis=1).astype(jnp.bfloat16)


def pack(value):
    both = value[:, :LANES] + value[:, LANES:]
    top, bottom = both[:LANES], both[LANES:]
    lower = lax.broadcasted_iota(jnp.int32, (LANES, LANES), 1) < RANK
    kept = jnp.where(lower, top, bottom)
    moved = pltpu.roll(jnp.where(lower, bottom, top), RANK, 1)
    return (kept + moved).reshape(16, 8, LANES)


def unpack_transposed(tiles):
    value = tiles.reshape(LANES, LANES).T
    return jnp.concatenate([value[:RANK], value[RANK:]], axis=1)


def fold(value):
    total = value[0:RANK]
    for i in range(1, PIECES):
        total = total + value[i * RANK : (i + 1) * RANK]
    return total


def to_tiles(value):
    parts = [
        value[:, l * LANES : (l + 1) * LANES].reshape(8, 8, LANES)
        for l in range(value.shape[1] // LANES)
    ]
    return jnp.concatenate(parts, axis=0)


def from_tiles(value):
    parts = [
        value[8 * l : 8 * l + 8].reshape(RANK, LANES)
        for l in range(value.shape[0] // 8)
    ]
    return jnp.concatenate(parts, axis=1)


def eliminate(work, first, last):
    lane = lax.broadcasted_iota(jnp.int32, (RANK, 2 * RANK), 1)
    row = lax.broadcasted_iota(jnp.int32, (RANK, 1), 0)
    lane1 = lax.broadcasted_iota(jnp.int32, (1, 2 * RANK), 1)

    def step(j, carry):
        a = work[...]
        pivot_row = work[pl.ds(j, 1), :]
        pivot = jnp.sum(jnp.where(lane1 == j, pivot_row, 0.0), axis=1, keepdims=True)
        column = jnp.sum(jnp.where(lane == j, a, 0.0), axis=1, keepdims=True)
        column = jnp.where(row > j, column, 0.0)
        work[...] = a - column * (pivot_row / pivot)
        return carry

    lax.fori_loop(first, last, step, 0)


def inverse_factor(work):
    a = work[...]
    lane = lax.broadcasted_iota(jnp.int32, (RANK, 2 * RANK), 1)
    row = lax.broadcasted_iota(jnp.int32, (RANK, 2 * RANK), 0)
    diagonal = jnp.sum(jnp.where(lane == row, a, 0.0), axis=1, keepdims=True)
    return a[:, RANK:] / jnp.sqrt(diagonal)


def kernel(
    g_hbm, e_hbm, q_ref, q_out, g, e, ph,
    qs, pp, sb, xs, xr, acc, yr, pg, qp, qr, qg, work,
    load_sem, sib_send, sib_recv, x_send, x_recv, y_send, y_recv,
    ag_send, ag_recv, xg_send, xg_recv, sg_send, sg_recv,
    qr_send, qr_recv, qa_send, qa_recv,
):
    dp = lax.axis_index("dp")
    t = lax.axis_index("tensor")
    y, z = lax.div(dp, NZ), lax.rem(dp, NZ)
    x, c = lax.div(t, 2), lax.rem(t, 2)
    sibling = (dp, t + 1 - 2 * c)

    def around(place, step, size):
        return lax.rem(place + step % size, size)

    xs_at = [around(x, d, NX) for d in range(NX)]
    ys_at = [around(y, d, NY) for d in range(NY)]
    zs_at = [around(z, d, NZ) for d in range(NZ)]

    odd = lax.rem(z, 2)
    odds = (odd, 1 - odd)

    def device(y_at, z_at, x_at):
        return (y_at * NZ + z_at, 2 * x_at + c)

    def either(k, even_case, odd_case):
        return even_case * (1 - odds[k]) + odd_case * odds[k]

    line_place = [[either(k, xs_at[d], ys_at[d]) for d in range(NX)] for k in (0, 1)]
    plane_place = [line_place[1], line_place[0]]
    line_device = [
        [device(either(k, y, ys_at[d]), z, either(k, xs_at[d], x)) for d in range(NX)]
        for k in (0, 1)
    ]

    def plane_device(k, du, dz):
        return device(either(k, ys_at[du], y), zs_at[dz], either(k, x, xs_at[du]))

    own_plane = {o: plane_device(0, *o) for o in OFFSETS}
    other_plane = {o: plane_device(1, *o) for o in OFFSETS}
    dp_peers = [device(ys_at[o[0]], zs_at[o[1]], x) for o in OFFSETS]

    everyone = []
    for o in OFFSETS:
        everyone.append(own_plane[o])
        if o[0]:
            everyone.append(other_plane[o])
    everyone.append(sibling)

    barrier = pltpu.get_barrier_semaphore()
    for peer in everyone:
        pl.semaphore_signal(barrier, inc=1, device_id=peer, device_id_type=MESH)

    def rows_of(core, slot):
        start = (core * NZ + zs_at[SLOTS[slot]]) * ROWS
        return pl.ds(pl.multiple_of(start, ROWS), ROWS)

    loads = []
    for slot in range(NZ):
        copies = []
        for i, core in enumerate((1 - c, c)):
            rows = rows_of(core, slot)
            for k, (hbm, vmem) in enumerate(((g_hbm, g), (e_hbm, e))):
                copy = pltpu.make_async_copy(
                    hbm.at[0, rows, :], vmem.at[rows, :], load_sem.at[slot, 2 * i + k]
                )
                copy.start()
                copies.append(copy)
        loads.append(copies)

    qs[...] = right_factor(q_ref[...])

    def send(src, dst, send_sem, recv_sem, target):
        pltpu.make_async_remote_copy(
            src_ref=src,
            dst_ref=dst,
            send_sem=send_sem,
            recv_sem=recv_sem,
            device_id=target,
            device_id_type=MESH,
        ).start()

    def wait_bytes(ref, sem):
        pltpu.make_async_copy(ref, ref, sem).wait()

    scale = 1.0 / N_DP
    for it in range(ITERS):

        def p_rows(core, slot):
            rows = rows_of(core, slot)
            factor = qs[...]
            a = jnp.dot(g[rows, :], factor, preferred_element_type=jnp.float32)
            b = jnp.dot(e[rows, :], factor, preferred_element_type=jnp.float32)
            return pack(a + b)

        def for_sibling(span):
            for slot in range(*SPANS[span]):
                pp[it, slot] = p_rows(1 - c, slot)

        def for_own(span):
            for slot in range(*SPANS[span]):
                xs[it, slot] = p_rows(c, slot)

        def slots(span):
            return pl.ds(SPANS[span][0], SPANS[span][1] - SPANS[span][0])

        def to_sibling(span):
            send(
                pp.at[it, slots(span)],
                sb.at[it, slots(span)],
                sib_send.at[it],
                sib_recv.at[it, span],
                sibling,
            )

        def to_line(span):
            wait_bytes(sb.at[it, slots(span)], sib_recv.at[it, span])
            for slot in range(*SPANS[span]):
                xs[it, slot] = xs[it, slot] + sb[it, slot]
            k = span % 2
            for d in (2, 1, 3):
                send(
                    xs.at[it, slots(span), pl.ds(4 * line_place[k][d], 4)],
                    xr.at[it, d - 1, slots(span)],
                    x_send.at[it],
                    x_recv.at[it, span],
                    line_device[k][d],
                )

        def to_plane(span):
            wait_bytes(xr.at[it, :, slots(span)], x_recv.at[it, span])
            k = span % 2
            for slot in range(*SPANS[span]):
                total = xs[it, slot, pl.ds(4 * line_place[k][0], 4)]
                for d in (1, 2, 3):
                    total = total + xr[it, d - 1, slot]
                acc[it, slot] = total * scale
            for du in (2, 1, 3, 0):
                for slot in range(*SPANS[span]):
                    o = (du, SLOTS[slot])
                    if o == (0, 0):
                        continue
                    send(
                        acc.at[it, slot, plane_place[k][du]],
                        yr.at[it, OFFSETS.index(o)],
                        y_send.at[it],
                        y_recv.at[it],
                        (own_plane, other_plane)[k][o],
                    )

        if it == 0:
            for span in range(N_SPANS):
                for slot in range(*SPANS[span]):
                    for copy in loads[slot]:
                        copy.wait()
                for_sibling(span)
                for_own(span)
            pl.semaphore_wait(barrier, len(everyone))
            for span in range(N_SPANS):
                to_sibling(span)
            to_line(0)
            to_line(1)
            to_line(2)
            to_plane(0)
            to_line(3)
            to_plane(1)
            to_line(4)
        else:
            for span in range(N_SPANS):
                for_sibling(span)
                to_sibling(span)
                for_own(span)
                if span:
                    to_line(span - 1)
                if span == 3:
                    to_plane(0)
            to_plane(1)
            to_line(4)
        to_plane(2)
        to_plane(3)
        to_plane(4)

        near = slot_of(0)
        mine = 4 * line_place[0][0] + plane_place[0][0]
        own = acc[it, near, plane_place[0][0]]
        wait_bytes(yr.at[it], y_recv.at[it])
        pg[it, c, near, mine] = own + jnp.sum(yr[it], axis=0)

        for o in OFFSETS:
            send(
                pg.at[it, c, near, mine],
                pg.at[it, c, slot_of(-o[1]), mine],
                ag_send.at[it],
                ag_recv.at[it, span_of(o[1])],
                own_plane[o],
            )

        for span in range(N_SPANS - 1, -1, -1):
            k = span % 2
            tiles = pg.at[it, c, slots(span), pl.ds(4 * line_place[k][0], 4)]
            if span == N_SPANS - 1:
                wait_bytes(yr.at[it, pl.ds(0, 3)], ag_recv.at[it, span])
            else:
                wait_bytes(tiles, ag_recv.at[it, span])
            for d in (2, 1, 3):
                send(
                    tiles, tiles, xg_send.at[it], xg_recv.at[it, span], line_device[k][d]
                )

        q_acc = jnp.zeros((RANK, COLS), jnp.float32)
        gram = jnp.zeros((PIECES * RANK, PIECES * RANK), jnp.float32)

        def q_rows(core, span, q_acc, gram):
            for slot in range(*SPANS[span]):
                rows = rows_of(core, slot)
                lhs = split(unpack_transposed(pg[it, core, slot]))
                a = jnp.dot(lhs, g[rows, :], preferred_element_type=jnp.float32)
                b = jnp.dot(lhs, e[rows, :], preferred_element_type=jnp.float32)
                more = lax.dot_general(
                    lhs, lhs, NT, preferred_element_type=jnp.float32
                )
                q_acc, gram = q_acc + fold(a + b), gram + more
            return q_acc, gram

        for span in range(N_SPANS - 1, -1, -1):
            wait_bytes(xr.at[it, :, slots(span)], xg_recv.at[it, span])
            chunk = pg.at[it, c, slots(span)]
            send(chunk, chunk, sg_send.at[it], sg_recv.at[it, span], sibling)
            q_acc, gram = q_rows(c, span, q_acc, gram)
        for span in range(N_SPANS - 1, -1, -1):
            wait_bytes(pg.at[it, 1 - c, slots(span)], sg_recv.at[it, span])
            q_acc, gram = q_rows(1 - c, span, q_acc, gram)

        qp[it] = to_tiles(q_acc * scale)
        for k, peer in enumerate(dp_peers):
            send(
                qp.at[it, peer[0]],
                qr.at[it, k],
                qr_send.at[it],
                qr_recv.at[it],
                peer,
            )

        square = jnp.zeros((RANK, RANK), jnp.float32)
        for i in range(PIECES):
            for j in range(PIECES):
                square = square + gram[
                    i * RANK : (i + 1) * RANK, j * RANK : (j + 1) * RANK
                ]
        row = lax.broadcasted_iota(jnp.int32, (RANK, RANK), 0)
        lane = lax.broadcasted_iota(jnp.int32, (RANK, RANK), 1)
        eye = jnp.where(row == lane, 1.0, 0.0)
        work[...] = jnp.concatenate([square, eye], axis=1)
        eliminate(work, 0, EARLY)

        wait_bytes(qr.at[it], qr_recv.at[it])
        qg[it, dp] = qp[it, dp] + jnp.sum(qr[it], axis=0)
        for peer in dp_peers:
            send(
                qg.at[it, dp],
                qg.at[it, dp],
                qa_send.at[it],
                qa_recv.at[it],
                peer,
            )
        eliminate(work, EARLY, RANK)
        l_inverse = inverse_factor(work)

        if it == ITERS - 1:
            none = jnp.zeros((RANK, RANK), jnp.float32)
            twice = jnp.concatenate(
                [
                    jnp.concatenate([l_inverse, none], axis=1),
                    jnp.concatenate([none, l_inverse], axis=1),
                ],
                axis=0,
            )
            lower = lax.broadcasted_iota(jnp.int32, (LANES, LANES), 1) < RANK
            for i in range(2 * NZ):
                hat = lax.dot_general(
                    pg[it, i // NZ, i % NZ].reshape(LANES, LANES),
                    twice,
                    NT,
                    precision=HIGH,
                    preferred_element_type=jnp.float32,
                )
                high = hat.astype(jnp.bfloat16).astype(jnp.float32)
                low = hat - high
                top = jnp.where(lower, high, pltpu.roll(low, RANK, 1))
                bottom = jnp.where(lower, pltpu.roll(high, RANK, 1), low)
                both = jnp.concatenate([top, bottom], axis=0).astype(jnp.bfloat16)
                ph[rows_of(i // NZ, i % NZ), :] = jnp.concatenate([both, both], axis=1)

        wait_bytes(pp.at[it], sib_send.at[it])
        wait_bytes(xr.at[it], x_send.at[it])
        wait_bytes(yr.at[it], y_send.at[it])
        wait_bytes(yr.at[it], ag_send.at[it])
        wait_bytes(xr.at[it], xg_send.at[it])
        wait_bytes(pp.at[it], sg_send.at[it])
        wait_bytes(qr.at[it], qr_send.at[it])

        wait_bytes(qr.at[it], qa_recv.at[it])
        q_now = jnp.dot(
            l_inverse,
            from_tiles(qg[it]),
            precision=HIGH,
            preferred_element_type=jnp.float32,
        )
        if it < ITERS - 1:
            qs[...] = right_factor(q_now)
        else:
            q_out[...] = q_now

    for it in range(ITERS):
        wait_bytes(qr.at[it], qa_send.at[it])


def finish(g, e, ph, q_ref, q_out, new_out, buffer, sem):
    copies = [pltpu.make_async_copy(q_ref, q_out, sem.at[2 * NZ])]
    copies[0].start()
    q_now = q_ref[...]
    high = q_now.astype(jnp.bfloat16)
    low = (q_now - high.astype(jnp.float32)).astype(jnp.bfloat16)
    right = jnp.concatenate([high, high, low, low], axis=0)
    for i in range(2 * NZ):
        rows = slice(i * ROWS, (i + 1) * ROWS)
        approx = jnp.dot(ph[rows, :], right, preferred_element_type=jnp.float32)
        merged = g[rows, :].astype(jnp.float32) + e[rows, :].astype(jnp.float32)
        buffer[rows, :] = (merged - approx).astype(jnp.bfloat16)
        copy = pltpu.make_async_copy(
            buffer.at[rows, :], new_out.at[0, rows, :], sem.at[i]
        )
        copy.start()
        copies.append(copy)
    for copy in copies:
        copy.wait()


def body(gradient, error, q_prev):
    f32, bf16 = jnp.float32, jnp.bfloat16
    dma = pltpu.SemaphoreType.DMA
    vmem = pl.BlockSpec(memory_space=pltpu.VMEM)
    hbm = pl.BlockSpec(memory_space=pltpu.HBM)
    q_t, g, e, p_hat = pl.pallas_call(
        kernel,
        out_shape=(
            jax.ShapeDtypeStruct((RANK, COLS), f32),
            jax.ShapeDtypeStruct((N, COLS), bf16),
            jax.ShapeDtypeStruct((N, COLS), bf16),
            jax.ShapeDtypeStruct((N, 4 * RANK), bf16),
        ),
        in_specs=[hbm, hbm, vmem],
        out_specs=(vmem, vmem, vmem, vmem),
        scratch_shapes=[
            pltpu.VMEM((COLS, 4 * RANK), bf16),
            pltpu.VMEM((ITERS, NZ, 16, 8, LANES), f32),
            pltpu.VMEM((ITERS, NZ, 16, 8, LANES), f32),
            pltpu.VMEM((ITERS, NZ, 16, 8, LANES), f32),
            pltpu.VMEM((ITERS, 3, NZ, 4, 8, LANES), f32),
            pltpu.VMEM((ITERS, NZ, 4, 8, LANES), f32),
            pltpu.VMEM((ITERS, N_DP - 1, 8, LANES), f32),
            pltpu.VMEM((ITERS, 2, NZ, 16, 8, LANES), f32),
            pltpu.VMEM((ITERS, N_DP, 8, LANES), f32),
            pltpu.VMEM((ITERS, N_DP - 1, 8, LANES), f32),
            pltpu.VMEM((ITERS, N_DP, 8, LANES), f32),
            pltpu.VMEM((RANK, 2 * RANK), f32),
            dma((NZ, 4)),
            dma((ITERS,)),
            dma((ITERS, N_SPANS)),
            dma((ITERS,)),
            dma((ITERS, N_SPANS)),
            dma((ITERS,)),
            dma((ITERS,)),
            dma((ITERS,)),
            dma((ITERS, N_SPANS)),
            dma((ITERS,)),
            dma((ITERS, N_SPANS)),
            dma((ITERS,)),
            dma((ITERS, N_SPANS)),
            dma((ITERS,)),
            dma((ITERS,)),
            dma((ITERS,)),
            dma((ITERS,)),
        ],
        compiler_params=pltpu.CompilerParams(
            collective_id=1, has_side_effects=True, vmem_limit_bytes=41 * 2**20
        ),
    )(gradient, error, q_prev.T)
    q_t, new_error = pl.pallas_call(
        finish,
        out_shape=(
            jax.ShapeDtypeStruct((RANK, COLS), f32),
            jax.ShapeDtypeStruct((1, N, COLS), bf16),
        ),
        in_specs=[vmem, vmem, vmem, vmem],
        out_specs=(
            pl.BlockSpec(memory_space=pl.ANY),
            pl.BlockSpec(memory_space=pl.ANY),
        ),
        scratch_shapes=[pltpu.VMEM((N, COLS), bf16), dma((2 * NZ + 1,))],
        compiler_params=pltpu.CompilerParams(vmem_limit_bytes=40 * 2**20),
    )(g, e, p_hat, q_t)
    return q_t.T, new_error


def solution(mesh):
    return jax.shard_map(
        body,
        mesh=mesh,
        in_specs=(P("dp", None, "tensor"), P("dp", None, "tensor"), P("tensor", None)),
        out_specs=(P("tensor", None), P("dp", None, "tensor")),
        check_vma=False,
    )
```

time: 96.1 us -> 92.9 us (0.967)
  Pallas kernels: 94.4 us -> 90.9 us
    pallas_call x1, Pallas kernels: 4.75 us -> 2.39 us  [body(): pl.pallas_call(finish, out_shape=(jax.ShapeDtypeStruct((RANK, COLS), f32)...]
    pallas_call x1, Pallas kernels: 89.6 us -> 88.5 us  [body(): pl.pallas_call(kernel, out_shape=(jax.ShapeDtypeStruct((RANK, COLS), f32)...]
where the time goes in v4:
time: 92.9 us; the launch traced here: 92.6 us
  Pallas kernels  90.9 us (98%)
    pallas_call x1, Pallas kernels, body(): pl.pallas_call(kernel, out_shape=(jax.ShapeDtypeStruct((RANK, COLS), f32)...  88.5 us
    pallas_call x1, Pallas kernels, body(): pl.pallas_call(finish, out_shape=(jax.ShapeDtypeStruct((RANK, COLS), f32)...  2.39 us

profile of v4, /device:TPU:2, one launch (start us, length us, event | category | flops | bytes accessed | tf_op | source)
XLA Modules:
  0.0 92.6 jit_solution(14534111784875749738)
XLA Ops:
  0.6 0.0 copy-start
  0.6 0.9 copy-done
  1.5 88.5 %shard_map.50 = (f32[64,512]{1,0:T(8,128)S(1)}, bf16[4096,512]{1,0:T(8,128)(2,1)S(1)}, bf16[4096,512]{1,0:T(8,128)(2,1)S(1)}, bf16[4096,256]{1,0:T(8,128)(2,1)S(1)}) custom-call(bf16[1,4096,512]{2,1,0:T(8,128)(2,1)} %g_hbm.1, bf16[1,4096,512]{2,1,0:T(8,128)(2,1)} %e_hbm.1, f32[64,512]{1,0:T(8,128)S(1)} %bitcast.2), custom_call_target="tpu_custom_call" | custom-call | tf_op jit(solution)/shard_map/pallas_call | solution.py:477
  90.1 2.4 %shard_map.51 = (f32[64,512]{1,0:T(8,128)}, bf16[1,4096,512]{2,1,0:T(8,128)(2,1)}) custom-call(bf16[4096,512]{1,0:T(8,128)(2,1)S(1)} %get-tuple-element.8.g, bf16[4096,512]{1,0:T(8,128)(2,1)S(1)} %get-tuple-element.9.e, bf16[4096,256]{1,0:T(8,128)(2,1)S(1)} %get-tuple-element.10.ph, f32[64,512]{1,0:T(8,128)S(1)} %get-tuple-element.11.q_ref), custom_call_target="tpu_custom_call" | custom-call | tf_op jit(solution)/shard_map/pallas_call | solution.py:522
Async XLA Ops:
  0.6 0.9 copy-start

commit v5 on v4

--- a/solution.py
+++ b/solution.py
@@ -17,6 +17,10 @@
 LANES = 128
 PIECES = 3
 EARLY = 48
+DIRECT = (0, 1)
+SKIP = (0, 1)
+SKIPPED = 3
+LAG = 5
 MESH = pl.DeviceIdType.MESH
 HIGH = lax.Precision.HIGHEST
 NT = (((1,), (1,)), ((), ()))
@@ -132,8 +136,8 @@
 
 def kernel(
     g_hbm, e_hbm, q_ref, q_out, g, e, ph,
-    qs, pp, sb, xs, xr, acc, yr, pg, qp, qr, qg, work,
-    load_sem, sib_send, sib_recv, x_send, x_recv, y_send, y_recv,
+    qs, pp, sb, xs, xr, x2r, acc, yr, pg, qp, qr, qg, work,
+    load_sem, sib_send, sib_recv, x_send, x_recv, x2_send, x2_recv, y_send, y_recv,
     ag_send, ag_recv, xg_send, xg_recv, sg_send, sg_recv,
     qr_send, qr_recv, qa_send, qa_recv,
 ):
@@ -166,6 +170,11 @@
         for k in (0, 1)
     ]
 
+    line_other_core = [
+        [(line_device[k][d][0], line_device[k][d][1] + 1 - 2 * c) for d in range(NX)]
+        for k in (0, 1)
+    ]
+
     def plane_device(k, du, dz):
         return device(either(k, ys_at[du], y), zs_at[dz], either(k, x, xs_at[du]))
 
@@ -179,6 +188,7 @@
         if o[0]:
             everyone.append(other_plane[o])
     everyone.append(sibling)
+    everyone += [line_other_core[k][d] for k in (0, 1) for d in (1, 2, 3)]
 
     barrier = pltpu.get_barrier_semaphore()
     for peer in everyone:
@@ -238,6 +248,8 @@
             return pl.ds(SPANS[span][0], SPANS[span][1] - SPANS[span][0])
 
         def to_sibling(span):
+            if span in SKIP:
+                return
             send(
                 pp.at[it, slots(span)],
                 sb.at[it, slots(span)],
@@ -247,10 +259,20 @@
             )
 
         def to_line(span):
-            wait_bytes(sb.at[it, slots(span)], sib_recv.at[it, span])
-            for slot in range(*SPANS[span]):
-                xs[it, slot] = xs[it, slot] + sb[it, slot]
             k = span % 2
+            if span in SKIP:
+                for d in (2, 1, 3, 0):
+                    send(
+                        pp.at[it, slots(span), pl.ds(4 * line_place[k][d], 4)],
+                        x2r.at[it, d, slots(span)],
+                        x2_send.at[it],
+                        x2_recv.at[it, span],
+                        line_other_core[k][d],
+                    )
+            else:
+                wait_bytes(sb.at[it, slots(span)], sib_recv.at[it, span])
+                for slot in range(*SPANS[span]):
+                    xs[it, slot] = xs[it, slot] + sb[it, slot]
             for d in (2, 1, 3):
                 send(
                     xs.at[it, slots(span), pl.ds(4 * line_place[k][d], 4)],
@@ -262,11 +284,16 @@
 
         def to_plane(span):
             wait_bytes(xr.at[it, :, slots(span)], x_recv.at[it, span])
+            if span in SKIP:
+                wait_bytes(x2r.at[it, :, slots(span)], x2_recv.at[it, span])
             k = span % 2
             for slot in range(*SPANS[span]):
                 total = xs[it, slot, pl.ds(4 * line_place[k][0], 4)]
                 for d in (1, 2, 3):
                     total = total + xr[it, d - 1, slot]
+                if span in SKIP:
+                    for d in range(NX):
+                        total = total + x2r[it, d, slot]
                 acc[it, slot] = total * scale
             for du in (2, 1, 3, 0):
                 for slot in range(*SPANS[span]):
@@ -291,27 +318,24 @@
             pl.semaphore_wait(barrier, len(everyone))
             for span in range(N_SPANS):
                 to_sibling(span)
-            to_line(0)
-            to_line(1)
-            to_line(2)
-            to_plane(0)
-            to_line(3)
-            to_plane(1)
-            to_line(4)
+            for span in range(N_SPANS):
+                to_line(span)
         else:
-            for span in range(N_SPANS):
+            for span in SKIP:
+                for_sibling(span)
+                for_own(span)
+                to_line(span)
+            rest = [span for span in range(N_SPANS) if span not in SKIP]
+            for span in rest:
                 for_sibling(span)
                 to_sibling(span)
+            for i, span in enumerate(rest):
                 for_own(span)
-                if span:
-                    to_line(span - 1)
-                if span == 3:
-                    to_plane(0)
-            to_plane(1)
-            to_line(4)
-        to_plane(2)
-        to_plane(3)
-        to_plane(4)
+                if i:
+                    to_line(rest[i - 1])
+            to_line(rest[-1])
+        for span in range(N_SPANS):
+            to_plane(span)
 
         near = slot_of(0)
         mine = 4 * line_place[0][0] + plane_place[0][0]
@@ -339,6 +363,9 @@
                 send(
                     tiles, tiles, xg_send.at[it], xg_recv.at[it, span], line_device[k][d]
                 )
+            if span in DIRECT:
+                for target in [line_other_core[k][d] for d in (2, 1, 3)] + [sibling]:
+                    send(tiles, tiles, sg_send.at[it], sg_recv.at[it, span], target)
 
         q_acc = jnp.zeros((RANK, COLS), jnp.float32)
         gram = jnp.zeros((PIECES * RANK, PIECES * RANK), jnp.float32)
@@ -355,14 +382,20 @@
                 q_acc, gram = q_acc + fold(a + b), gram + more
             return q_acc, gram
 
+        def sibling_q(span, q_acc, gram):
+            wait_bytes(pg.at[it, 1 - c, slots(span)], sg_recv.at[it, span])
+            return q_rows(1 - c, span, q_acc, gram)
+
         for span in range(N_SPANS - 1, -1, -1):
             wait_bytes(xr.at[it, :, slots(span)], xg_recv.at[it, span])
-            chunk = pg.at[it, c, slots(span)]
-            send(chunk, chunk, sg_send.at[it], sg_recv.at[it, span], sibling)
+            if span not in DIRECT:
+                chunk = pg.at[it, c, slots(span)]
+                send(chunk, chunk, sg_send.at[it], sg_recv.at[it, span], sibling)
             q_acc, gram = q_rows(c, span, q_acc, gram)
-        for span in range(N_SPANS - 1, -1, -1):
-            wait_bytes(pg.at[it, 1 - c, slots(span)], sg_recv.at[it, span])
-            q_acc, gram = q_rows(1 - c, span, q_acc, gram)
+            if span + LAG < N_SPANS:
+                q_acc, gram = sibling_q(span + LAG, q_acc, gram)
+        for span in range(LAG - 1, -1, -1):
+            q_acc, gram = sibling_q(span, q_acc, gram)
 
         qp[it] = to_tiles(q_acc * scale)
         for k, peer in enumerate(dp_peers):
@@ -424,7 +457,8 @@
                 both = jnp.concatenate([top, bottom], axis=0).astype(jnp.bfloat16)
                 ph[rows_of(i // NZ, i % NZ), :] = jnp.concatenate([both, both], axis=1)
 
-        wait_bytes(pp.at[it], sib_send.at[it])
+        wait_bytes(pp.at[it, pl.ds(SKIPPED, NZ - SKIPPED)], sib_send.at[it])
+        wait_bytes(x2r.at[it], x2_send.at[it])
         wait_bytes(xr.at[it], x_send.at[it])
         wait_bytes(yr.at[it], y_send.at[it])
         wait_bytes(yr.at[it], ag_send.at[it])
@@ -490,6 +524,7 @@
             pltpu.VMEM((ITERS, NZ, 16, 8, LANES), f32),
             pltpu.VMEM((ITERS, NZ, 16, 8, LANES), f32),
             pltpu.VMEM((ITERS, 3, NZ, 4, 8, LANES), f32),
+            pltpu.VMEM((ITERS, NX, SKIPPED, 4, 8, LANES), f32),
             pltpu.VMEM((ITERS, NZ, 4, 8, LANES), f32),
             pltpu.VMEM((ITERS, N_DP - 1, 8, LANES), f32),
             pltpu.VMEM((ITERS, 2, NZ, 16, 8, LANES), f32),
@@ -498,6 +533,8 @@
             pltpu.VMEM((ITERS, N_DP, 8, LANES), f32),
             pltpu.VMEM((RANK, 2 * RANK), f32),
             dma((NZ, 4)),
+            dma((ITERS,)),
+            dma((ITERS, N_SPANS)),
             dma((ITERS,)),
             dma((ITERS, N_SPANS)),
             dma((ITERS,)),

time: 92.9 us -> 89.6 us (0.964)
  Pallas kernels: 90.9 us -> 87.8 us
    pallas_call x1, Pallas kernels: 88.5 us -> 85.4 us  [body(): pl.pallas_call(kernel, out_shape=(jax.ShapeDtypeStruct((RANK, COLS), f32)...]
where the time goes in v5:
time: 89.6 us; the launch traced here: 89.5 us
  Pallas kernels  87.8 us (98%)
  local copies, waits for them, and re-layouts  0.9 us (1%)
    pallas_call x1, Pallas kernels, body(): pl.pallas_call(kernel, out_shape=(jax.ShapeDtypeStruct((RANK, COLS), f32)...  85.4 us
    pallas_call x1, Pallas kernels, body(): pl.pallas_call(finish, out_shape=(jax.ShapeDtypeStruct((RANK, COLS), f32)...  2.39 us

profile of v5, /device:TPU:2, one launch (start us, length us, event | category | flops | bytes accessed | tf_op | source)
XLA Modules:
  0.0 89.5 jit_solution(15245387367515581665)
XLA Ops:
  0.6 0.0 copy-start
  0.6 0.9 %copy-done = f32[512,64]{0,1:T(8,128)S(1)} copy-done((f32[512,64]{0,1:T(8,128)S(1)}, f32[512,64]{0,1:T(8,128)}, u32[]{:S(2)}) %copy-start) | copy-done | bytes 131096
  1.5 85.4 %shard_map.50 = (f32[64,512]{1,0:T(8,128)S(1)}, bf16[4096,512]{1,0:T(8,128)(2,1)S(1)}, bf16[4096,512]{1,0:T(8,128)(2,1)S(1)}, bf16[4096,256]{1,0:T(8,128)(2,1)S(1)}) custom-call(bf16[1,4096,512]{2,1,0:T(8,128)(2,1)} %g_hbm.1, bf16[1,4096,512]{2,1,0:T(8,128)(2,1)} %e_hbm.1, f32[64,512]{1,0:T(8,128)S(1)} %bitcast.2), custom_call_target="tpu_custom_call" | custom-call | tf_op jit(solution)/shard_map/pallas_call | solution.py:511
  86.9 2.4 %shard_map.51 = (f32[64,512]{1,0:T(8,128)}, bf16[1,4096,512]{2,1,0:T(8,128)(2,1)}) custom-call(bf16[4096,512]{1,0:T(8,128)(2,1)S(1)} %get-tuple-element.8.g, bf16[4096,512]{1,0:T(8,128)(2,1)S(1)} %get-tuple-element.9.e, bf16[4096,256]{1,0:T(8,128)(2,1)S(1)} %get-tuple-element.10.ph, f32[64,512]{1,0:T(8,128)S(1)} %get-tuple-element.11.q_ref), custom_call_target="tpu_custom_call" | custom-call | tf_op jit(solution)/shard_map/pallas_call | solution.py:559
Async XLA Ops:
  0.6 0.9 %copy-start = (f32[512,64]{0,1:T(8,128)S(1)}, f32[512,64]{0,1:T(8,128)}, u32[]{:S(2)}) copy-start(f32[512,64]{0,1:T(8,128)} %param.5) | copy-start | bytes 393220

commit v6 on v5

--- a/solution.py
+++ b/solution.py
@@ -16,11 +16,10 @@
 COLS = N // N_T
 LANES = 128
 PIECES = 3
-EARLY = 48
-DIRECT = (0, 1)
+EARLY = 40
+DIRECT = (0, 1, 2)
 SKIP = (0, 1)
 SKIPPED = 3
-LAG = 5
 MESH = pl.DeviceIdType.MESH
 HIGH = lax.Precision.HIGHEST
 NT = (((1,), (1,)), ((), ()))
@@ -38,6 +37,8 @@
     [(du, dz) for du in range(NY) for dz in range(NZ) if du or dz],
     key=lambda o: -distance(o),
 )
+GATHER_ORDER = [o for o in OFFSETS if not o[1]] + [o for o in OFFSETS if o[1]]
+
 SLOTS = (4, 3, 5, 2, 6, 1, 7, 0)
 SPANS = ((0, 1), (1, 3), (3, 5), (5, 7), (7, 8))
 N_SPANS = len(SPANS)
@@ -136,7 +137,7 @@
 
 def kernel(
     g_hbm, e_hbm, q_ref, q_out, g, e, ph,
-    qs, pp, sb, xs, xr, x2r, acc, yr, pg, qp, qr, qg, work,
+    qs, pp, sb, xs, xr, x2r, acc, yr, pg, ps, qp, qr, qg, work,
     load_sem, sib_send, sib_recv, x_send, x_recv, x2_send, x2_recv, y_send, y_recv,
     ag_send, ag_recv, xg_send, xg_recv, sg_send, sg_recv,
     qr_send, qr_recv, qa_send, qa_recv,
@@ -343,7 +344,7 @@
         wait_bytes(yr.at[it], y_recv.at[it])
         pg[it, c, near, mine] = own + jnp.sum(yr[it], axis=0)
 
-        for o in OFFSETS:
+        for o in GATHER_ORDER:
             send(
                 pg.at[it, c, near, mine],
                 pg.at[it, c, slot_of(-o[1]), mine],
@@ -368,34 +369,27 @@
                     send(tiles, tiles, sg_send.at[it], sg_recv.at[it, span], target)
 
         q_acc = jnp.zeros((RANK, COLS), jnp.float32)
-        gram = jnp.zeros((PIECES * RANK, PIECES * RANK), jnp.float32)
-
-        def q_rows(core, span, q_acc, gram):
+
+        def q_rows(core, place, span, q_acc):
             for slot in range(*SPANS[span]):
                 rows = rows_of(core, slot)
                 lhs = split(unpack_transposed(pg[it, core, slot]))
+                start = (place * NZ + slot) * ROWS
+                ps[:, start : start + ROWS] = lhs
                 a = jnp.dot(lhs, g[rows, :], preferred_element_type=jnp.float32)
                 b = jnp.dot(lhs, e[rows, :], preferred_element_type=jnp.float32)
-                more = lax.dot_general(
-                    lhs, lhs, NT, preferred_element_type=jnp.float32
-                )
-                q_acc, gram = q_acc + fold(a + b), gram + more
-            return q_acc, gram
-
-        def sibling_q(span, q_acc, gram):
-            wait_bytes(pg.at[it, 1 - c, slots(span)], sg_recv.at[it, span])
-            return q_rows(1 - c, span, q_acc, gram)
+                q_acc = q_acc + fold(a + b)
+            return q_acc
 
         for span in range(N_SPANS - 1, -1, -1):
             wait_bytes(xr.at[it, :, slots(span)], xg_recv.at[it, span])
             if span not in DIRECT:
                 chunk = pg.at[it, c, slots(span)]
                 send(chunk, chunk, sg_send.at[it], sg_recv.at[it, span], sibling)
-            q_acc, gram = q_rows(c, span, q_acc, gram)
-            if span + LAG < N_SPANS:
-                q_acc, gram = sibling_q(span + LAG, q_acc, gram)
-        for span in range(LAG - 1, -1, -1):
-            q_acc, gram = sibling_q(span, q_acc, gram)
+            q_acc = q_rows(c, 0, span, q_acc)
+        for span in range(N_SPANS - 1, -1, -1):
+            wait_bytes(pg.at[it, 1 - c, slots(span)], sg_recv.at[it, span])
+            q_acc = q_rows(1 - c, 1, span, q_acc)
 
         qp[it] = to_tiles(q_acc * scale)
         for k, peer in enumerate(dp_peers):
@@ -407,6 +401,9 @@
                 peer,
             )
 
+        gram = lax.dot_general(
+            ps[...], ps[...], NT, preferred_element_type=jnp.float32
+        )
         square = jnp.zeros((RANK, RANK), jnp.float32)
         for i in range(PIECES):
             for j in range(PIECES):
@@ -528,6 +525,7 @@
             pltpu.VMEM((ITERS, NZ, 4, 8, LANES), f32),
             pltpu.VMEM((ITERS, N_DP - 1, 8, LANES), f32),
             pltpu.VMEM((ITERS, 2, NZ, 16, 8, LANES), f32),
+            pltpu.VMEM((PIECES * RANK, N), bf16),
             pltpu.VMEM((ITERS, N_DP, 8, LANES), f32),
             pltpu.VMEM((ITERS, N_DP - 1, 8, LANES), f32),
             pltpu.VMEM((ITERS, N_DP, 8, LANES), f32),

time: 89.6 us -> 89 us (level)
  Pallas kernels: 87.8 us -> 86.7 us
    pallas_call x1, Pallas kernels: 85.4 us -> 84.3 us  [body(): pl.pallas_call(kernel, out_shape=(jax.ShapeDtypeStruct((RANK, COLS), f32)...]
where the time goes in v6:
time: 89 us; the launch traced here: 88.4 us
  Pallas kernels  86.7 us (97%)
  local copies, waits for them, and re-layouts  0.9 us (1%)
    pallas_call x1, Pallas kernels, body(): pl.pallas_call(kernel, out_shape=(jax.ShapeDtypeStruct((RANK, COLS), f32)...  84.3 us
    pallas_call x1, Pallas kernels, body(): pl.pallas_call(finish, out_shape=(jax.ShapeDtypeStruct((RANK, COLS), f32)...  2.39 us

profile of v6, /device:TPU:2, one launch (start us, length us, event | category | flops | bytes accessed | tf_op | source)
XLA Modules:
  0.0 88.4 jit_solution(16007472041063052620)
XLA Ops:
  0.6 0.0 copy-start
  0.6 0.9 %copy-done = f32[512,64]{0,1:T(8,128)S(1)} copy-done((f32[512,64]{0,1:T(8,128)S(1)}, f32[512,64]{0,1:T(8,128)}, u32[]{:S(2)}) %copy-start) | copy-done | bytes 131096
  1.5 84.3 %shard_map.50 = (f32[64,512]{1,0:T(8,128)S(1)}, bf16[4096,512]{1,0:T(8,128)(2,1)S(1)}, bf16[4096,512]{1,0:T(8,128)(2,1)S(1)}, bf16[4096,256]{1,0:T(8,128)(2,1)S(1)}) custom-call(bf16[1,4096,512]{2,1,0:T(8,128)(2,1)} %g_hbm.1, bf16[1,4096,512]{2,1,0:T(8,128)(2,1)} %e_hbm.1, f32[64,512]{1,0:T(8,128)S(1)} %bitcast.2), custom_call_target="tpu_custom_call" | custom-call | tf_op jit(solution)/shard_map/pallas_call | solution.py:508
  85.9 2.4 %shard_map.51 = (f32[64,512]{1,0:T(8,128)}, bf16[1,4096,512]{2,1,0:T(8,128)(2,1)}) custom-call(bf16[4096,512]{1,0:T(8,128)(2,1)S(1)} %get-tuple-element.8.g, bf16[4096,512]{1,0:T(8,128)(2,1)S(1)} %get-tuple-element.9.e, bf16[4096,256]{1,0:T(8,128)(2,1)S(1)} %get-tuple-element.10.ph, f32[64,512]{1,0:T(8,128)S(1)} %get-tuple-element.11.q_ref), custom_call_target="tpu_custom_call" | custom-call | tf_op jit(solution)/shard_map/pallas_call | solution.py:557
Async XLA Ops:
  0.6 0.9 %copy-start = (f32[512,64]{0,1:T(8,128)S(1)}, f32[512,64]{0,1:T(8,128)}, u32[]{:S(2)}) copy-start(f32[512,64]{0,1:T(8,128)} %param.5) | copy-start | bytes 393220
